TPU v7x, 128 devices: a whole 4x4x4 slice. The times are simulated.
128 devices in a mesh: grp: 4 (over z_lo, core), wf: 32 (over x, z_hi, y).
Axes of the slice: x: 4, y: 4, z: 4 (z_hi: 2, z_lo: 2; z = z_hi * 2 + z_lo), core: 2. Of those that a mesh axis runs over, the one named last changes fastest.
Arguments:
- quasi: float32 [128, 4, 262144], P(('grp', 'wf')), may hold values from -6 to 6
- outer_field: float32 [262144], replicated, may hold values from -4 to 4
- coupling: float32 [262144], replicated, may hold values from 2 to 16
Outputs:
- evolved: float32 [128, 4, 262144], P(('grp', 'wf'))
- potentials: float32 [3, 64, 4096], P(None, 'grp', 'wf')
All inputs are finite; a program needn't handle non-finite values.
Results may differ from a plain program's by a relative error of at most 0.0003.
Values sent between devices are 32-bit elements; how exact they have to be, the bound alone decides.
A program may use at most 192 MiB of HBM per device.

v0:
```python
import math

import jax
import jax.numpy as jnp
from jax import lax
from jax.sharding import PartitionSpec as P

NX = 64
NG = 64


time_step = 0.2
kinetic_coef = 0.5
density_coef = 1.0
coulomb_coef = 0.25


def neighbour_sum(field, first, grid):
    positions = jnp.arange(first * grid * grid, dtype=jnp.int32)
    depth_index = positions % grid
    column_index = positions // grid % grid
    plane = grid * grid
    total = jnp.roll(field, plane, -1) + jnp.roll(field, -plane, -1)
    total = total + jnp.where(
        column_index == grid - 1, jnp.roll(field, (grid - 1) * grid, -1), jnp.roll(field, -grid, -1)
    )
    total = total + jnp.where(
        column_index == 0, jnp.roll(field, -(grid - 1) * grid, -1), jnp.roll(field, grid, -1)
    )
    total = total + jnp.where(
        depth_index == grid - 1, jnp.roll(field, grid - 1, -1), jnp.roll(field, -1, -1)
    )
    total = total + jnp.where(
        depth_index == 0, jnp.roll(field, 1 - grid, -1), jnp.roll(field, 1, -1)
    )
    return total - 6.0 * field


def hamiltonian(state, laplace, fields):
    mean_field, pair_real, pair_imag = (fields[0], fields[1], fields[2])
    single = -kinetic_coef * laplace + mean_field * state
    first = single[..., 0, :] + pair_real * state[..., 2, :] - pair_imag * state[..., 3, :]
    second = single[..., 1, :] + pair_real * state[..., 3, :] + pair_imag * state[..., 2, :]
    third = pair_real * state[..., 0, :] + pair_imag * state[..., 1, :] - single[..., 2, :]
    fourth = pair_real * state[..., 1, :] - pair_imag * state[..., 0, :] - single[..., 3, :]
    return jnp.stack([first, second, third, fourth], axis=-2)


def propagate(state, laplace, fields, first, grid):
    result = state
    term = state
    for degree in range(1, 5):
        current = laplace if degree == 1 else neighbour_sum(term, first, grid)
        applied = hamiltonian(term, current, fields)
        factor = time_step / degree
        term = jnp.stack(
            [
                factor * applied[..., 1, :],
                -factor * applied[..., 0, :],
                factor * applied[..., 3, :],
                -factor * applied[..., 2, :],
            ],
            axis=-2,
        )
        result = result + term
    return result


def lattice_symbol(indices, length):
    return 2.0 - 2.0 * jnp.cos(2.0 * math.pi / length * indices.astype(jnp.float32))


def coulomb_kernel(first_index, second_index, third_index, first_len, grid):
    squared = (
        lattice_symbol(first_index, first_len)[:, None, None]
        + lattice_symbol(second_index, grid)[None, :, None]
        + lattice_symbol(third_index, grid)[None, None, :]
    )
    return jnp.where(
        squared > 0.001,
        4.0 * math.pi * coulomb_coef / jnp.where(squared > 0.001, squared, 1.0),
        0.0,
    )


def transform(real_part, imag_part, axis, inverse):
    length = real_part.shape[axis]
    series = jnp.arange(length, dtype=jnp.int32)
    angle = (
        2.0 * math.pi / length * (series[:, None] * series[None, :] % length).astype(jnp.float32)
    )
    cosine = jnp.cos(angle)
    sine = jnp.sin(angle)
    moved_real = jnp.moveaxis(real_part, axis, -1)
    moved_imag = jnp.moveaxis(imag_part, axis, -1)

    def apply(matrix, values):
        return jnp.dot(values, matrix, precision=lax.Precision.HIGHEST)

    if inverse:
        new_real = (apply(cosine, moved_real) - apply(sine, moved_imag)) / length
        new_imag = (apply(cosine, moved_imag) + apply(sine, moved_real)) / length
    else:
        new_real = apply(cosine, moved_real) + apply(sine, moved_imag)
        new_imag = apply(cosine, moved_imag) - apply(sine, moved_real)
    return (jnp.moveaxis(new_real, -1, axis), jnp.moveaxis(new_imag, -1, axis))


def local(quasi, outer_field, coupling):
    grid = NG
    first_len = NX
    waves_total = quasi.shape[0] * lax.axis_size("grp") * lax.axis_size("wf")
    laplace = neighbour_sum(quasi, first_len, grid)
    partial_value = (
        jnp.stack(
            [
                jnp.sum(quasi[:, 2] * quasi[:, 2] + quasi[:, 3] * quasi[:, 3], axis=0),
                jnp.sum(quasi[:, 0] * quasi[:, 2] + quasi[:, 1] * quasi[:, 3], axis=0),
                jnp.sum(quasi[:, 1] * quasi[:, 2] - quasi[:, 0] * quasi[:, 3], axis=0),
            ]
        )
        / waves_total
    )
    rows = first_len // lax.axis_size("grp")
    width = grid * grid // lax.axis_size("wf")
    row_start = lax.axis_index("grp") * rows
    col_start = lax.axis_index("wf") * width
    summed = lax.psum(partial_value, ("grp", "wf"))
    cube = summed[0].reshape(first_len, grid, grid)
    real_part, imag_part = transform(cube, jnp.zeros_like(cube), 2, False)
    real_part, imag_part = transform(real_part, imag_part, 1, False)
    real_part, imag_part = transform(real_part, imag_part, 0, False)
    series = jnp.arange(grid, dtype=jnp.int32)
    kernel = coulomb_kernel(jnp.arange(first_len, dtype=jnp.int32), series, series, first_len, grid)
    real_part, imag_part = transform(real_part * kernel, imag_part * kernel, 0, True)
    real_part, imag_part = transform(real_part, imag_part, 1, True)
    real_part, imag_part = transform(real_part, imag_part, 2, True)
    fields = jnp.stack(
        [
            outer_field + density_coef * summed[0] + real_part.reshape(-1),
            -coupling * summed[1],
            -coupling * summed[2],
        ]
    )
    potentials = lax.dynamic_slice(
        fields.reshape(3, first_len, grid * grid), (0, row_start, col_start), (3, rows, width)
    )
    evolved = propagate(quasi, laplace, fields, first_len, grid)
    return (evolved, potentials)


def solution(mesh):
    placed = (P(("grp", "wf"), None, None), P(), P())
    return jax.shard_map(
        local,
        mesh=mesh,
        in_specs=placed,
        out_specs=(P(("grp", "wf"), None, None), P(None, "grp", "wf")),
        check_vma=False,
    )
```

profile of v0, /device:TPU:1, one launch (start us, length us, event | category | flops | bytes accessed | tf_op | source)
XLA Modules:
  0.0 608.1 jit_solution(8856617666752826919)
XLA Ops:
  7.2 13.3 %fusion.256 = (f32[1,1,262144]{2,1,0:T(1,128)}, f32[1,262144]{1,0:T(1,128)S(1)}, f32[1,262144]{1,0:T(1,128)S(1)}, f32[1,262144]{1,0:T(1,128)S(1)}, f32[1,1,26214...) fusion(f32[1,4,262144]{2,1,0:T(4,128)} %param.3), kind=kLoop, calls=%fused_computation.304 | loop fusion | flops 2359296 | bytes 11534336 | tf_op jit(solution)/shard_map/slice | solution.py:118
  20.5 4.4 maximum_multiply_fusion
  24.9 6.7 %fusion.266 = (f32[1,4,258048]{2,1,0:T(4,128)}, f32[1,4,258048]{2,1,0:T(4,128)}) fusion(f32[1,4,262144]{2,1,0:T(4,128)} %param.3), kind=kLoop, calls=%fused_computation.314 | loop fusion | bytes 16515072 | tf_op jit(solution)/shard_map/jit(_roll_static)/slice | solution.py:23
  31.6 4.5 fusion.264
  36.2 4.5 fusion.263
  40.7 4.4 fusion.260
  45.3 4.5 fusion.259
  56.9 125.5 %all-reduce.2.cloned.1.call-done = f32[3,262144]{1,0:T(4,128)} async-done(((f32[3,262144]{1,0:T(4,128)}), f32[3,262144]{1,0:T(4,128)}) %all-reduce.2.cloned.1.call-update) | async-done | bytes 3145744 | tf_op jit(solution)/shard_map/psum | solution.py:128
  182.4 20.7 %fusion.257 = (f32[1,262144]{1,0:T(1,128)}, f32[262144]{0:T(1024)}, f32[1,262144]{1,0:T(1,128)}, f32[1,262144]{1,0:T(1,128)}) fusion(f32[3,262144]{1,0:T(4,128)} %all-reduce.2.cloned.1.call-done), kind=kLoop, calls=%fused_computation.305 | loop fusion | bytes 7340032 | tf_op jit(solution)/shard_map/slice | solution.py:142
  212.6 4.9 fusion.36
  219.7 4.8 subtract_bitcast_fusion
  228.7 5.0 fusion.90
  233.6 4.9 add_bitcast_fusion
  290.1 28.9 %fusion.6 = f32[1,4,262144]{2,1,0:T(4,128)} fusion(f32[1,4,258048]{2,1,0:T(4,128)} %get-tuple-element.123, f32[1,4,4096]{2,1,0:T(4,128)S(1)} %get-tuple-element.125, f32[1,4,4096]{2,1,0:T(4,128)S(1)} %get-tuple-element.124, f32[1,4,258048]{2,1,0:T(4,128)} %get-tuple-element.122, f32[1,4,258112]{2,1,0:T(4,128)} %get-tuple-element.119, ...), kind=kLoop, calls=%fused_computation.7 | loop fusion | flops 25165824 | bytes 52428800 | tf_op jit(solution)/shard_map/add | solution.py:41
  319.1 10.5 %fusion.255 = (f32[1,1,262144]{2,1,0:T(1,128)S(1)}, f32[1,1,262144]{2,1,0:T(1,128)S(1)}, f32[1,1,262144]{2,1,0:T(1,128)S(1)}, f32[1,1,262144]{2,1,0:T(1,128)S(1)}) fusion(f32[1,4,262144]{2,1,0:T(4,128)} %fusion.6), kind=kLoop, calls=%fused_computation.303 | loop fusion | bytes 8388608 | tf_op jit(solution)/shard_map/slice | solution.py:42
  339.4 4.4 fusion.251
  344.6 4.5 fusion.250
  349.1 4.8 fusion.247
  354.7 4.4 fusion.246
  359.1 41.1 %fusion.13 = f32[1,4,262144]{2,1,0:T(4,128)} fusion(f32[1,4,258048]{2,1,0:T(4,128)} %get-tuple-element.86, f32[1,4,4096]{2,1,0:T(4,128)S(1)} %get-tuple-element.88, f32[1,4,4096]{2,1,0:T(4,128)S(1)} %get-tuple-element.87, f32[1,4,258048]{2,1,0:T(4,128)} %get-tuple-element.85, f32[1,4,258112]{2,1,0:T(4,128)} %get-tuple-element.82, ...), kind=kLoop, calls=%fused_computation.21 | loop fusion | flops 28311552 | bytes 52428800 | tf_op jit(solution)/shard_map/add | solution.py:41
  400.2 10.5 %fusion.244 = (f32[1,1,262144]{2,1,0:T(1,128)S(1)}, f32[1,1,262144]{2,1,0:T(1,128)S(1)}, f32[1,1,262144]{2,1,0:T(1,128)S(1)}, f32[1,1,262144]{2,1,0:T(1,128)S(1)}) fusion(f32[1,4,262144]{2,1,0:T(4,128)} %fusion.13), kind=kLoop, calls=%fused_computation.292 | loop fusion | bytes 8388608 | tf_op jit(solution)/shard_map/slice | solution.py:43
  420.4 4.6 fusion.240
  425.8 4.5 fusion.239
  430.4 4.4 fusion.236
  439.9 41.1 %fusion.20 = f32[1,4,262144]{2,1,0:T(4,128)} fusion(f32[1,4,258048]{2,1,0:T(4,128)} %get-tuple-element.58, f32[1,4,4096]{2,1,0:T(4,128)S(1)} %get-tuple-element.60, f32[1,4,4096]{2,1,0:T(4,128)S(1)} %get-tuple-element.59, f32[1,4,258048]{2,1,0:T(4,128)} %get-tuple-element.57, f32[1,4,258112]{2,1,0:T(4,128)} %get-tuple-element.54, ...), kind=kLoop, calls=%fused_computation.34 | loop fusion | flops 28311552 | bytes 52428800 | tf_op jit(solution)/shard_map/add | solution.py:41
  481.1 10.5 %fusion.233 = (f32[1,1,262144]{2,1,0:T(1,128)S(1)}, f32[1,1,262144]{2,1,0:T(1,128)S(1)}, f32[1,1,262144]{2,1,0:T(1,128)S(1)}, f32[1,1,262144]{2,1,0:T(1,128)S(1)}) fusion(f32[1,4,262144]{2,1,0:T(4,128)} %fusion.20), kind=kLoop, calls=%fused_computation.281 | loop fusion | bytes 8388608 | tf_op jit(solution)/shard_map/slice | solution.py:43
  502.6 4.4 fusion.229
  507.9 4.5 fusion.228
  512.4 4.4 fusion.225
  526.7 41.1 %fusion.27 = f32[1,4,262144]{2,1,0:T(4,128)} fusion(f32[1,4,258048]{2,1,0:T(4,128)} %get-tuple-element.34, f32[1,4,4096]{2,1,0:T(4,128)S(1)} %get-tuple-element.36, f32[1,4,4096]{2,1,0:T(4,128)S(1)} %get-tuple-element.35, f32[1,4,258048]{2,1,0:T(4,128)} %get-tuple-element.33, f32[1,4,258112]{2,1,0:T(4,128)} %get-tuple-element.30, ...), kind=kLoop, calls=%fused_computation.47 | loop fusion | flops 28311552 | bytes 52428800 | tf_op jit(solution)/shard_map/add | solution.py:41
  567.8 11.5 %fusion.222 = (f32[1,1,262144]{2,1,0:T(1,128)S(1)}, f32[1,1,262144]{2,1,0:T(1,128)S(1)}, f32[1,1,262144]{2,1,0:T(1,128)S(1)}, f32[1,1,262144]{2,1,0:T(1,128)}) fusion(f32[1,4,262144]{2,1,0:T(4,128)} %fusion.27), kind=kLoop, calls=%fused_computation.270 | loop fusion | bytes 8388608 | tf_op jit(solution)/shard_map/slice | solution.py:43
  584.0 16.1 %maximum_add_fusion.4 = f32[1,4,262144]{2,1,0:T(4,128)} fusion(f32[1,1,262144]{2,1,0:T(1,128)S(1)} %bitcast.185, f32[1,1,262144]{2,1,0:T(1,128)S(1)} %bitcast.186, f32[1,1,262144]{2,1,0:T(1,128)S(1)} %bitcast.184, f32[1,1,262144]{2,1,0:T(1,128)S(1)} %bitcast.183, f32[1,4,262144]{2,1,0:T(4,128)S(1)} %copy-done.2, f32[1,1,262144]{2,1,0:T(1,128)S(1)} %bitcast.155, ...), kind=kLoop, calls=%fused_computation.52 | loop fusion | flops 16777216 | bytes 25165824 | tf_op jit(solution)/shard_map/add | solution.py:65
  (188 shorter events, 128.1 us)
Async XLA Ops:
  7.2 175.3 %all-reduce.2.cloned.1.call-start = ((), (), s32[]{:S(2)}) async-start(), calls=%async_computation | async-start | bytes 8388608 | tf_op jit(solution)/shard_map/psum | solution.py:128
  24.9 6.7 %copy-start = (f32[1,4,262144]{2,1,0:T(4,128)S(1)}, f32[1,4,262144]{2,1,0:T(4,128)}, u32[]{:S(2)}) copy-start(f32[1,4,262144]{2,1,0:T(4,128)} %param.3) | copy-start | bytes 12582916
  53.4 236.7 %copy-start.49 = (pred[262144]{0:T(1024)(128)(4,1)}, pred[262144]{0:T(1024)(128)(4,1)S(1)}, u32[]{:S(2)}) copy-start(pred[262144]{0:T(1024)(128)(4,1)S(1)} %get-tuple-element.134) | copy-start | bytes 786436
  54.3 235.8 %copy-start.50 = (pred[262144]{0:T(1024)(128)(4,1)}, pred[262144]{0:T(1024)(128)(4,1)S(1)}, u32[]{:S(2)}) copy-start(pred[262144]{0:T(1024)(128)(4,1)S(1)} %get-tuple-element.135) | copy-start | bytes 786436
  261.0 6.5 %copy-start.42 = (f32[64,64,64]{2,1,0:T(8,128)S(1)}, f32[64,64,64]{2,1,0:T(8,128)}, u32[]{:S(2)}) copy-start(f32[64,64,64]{2,1,0:T(8,128)} %fusion.86) | copy-start | bytes 3145732
  261.0 6.5 %copy-start.44 = (f32[64,64,64]{2,1,0:T(8,128)S(1)}, f32[64,64,64]{2,1,0:T(8,128)}, u32[]{:S(2)}) copy-start(f32[64,64,64]{2,1,0:T(8,128)} %copy-done.43) | copy-start | bytes 3145732
  319.0 10.6 %copy-start.39 = (f32[1,1,262144]{2,1,0:T(1,128)S(1)}, f32[1,1,262144]{2,1,0:T(1,128)}, u32[]{:S(2)}) copy-start(f32[1,1,262144]{2,1,0:T(1,128)} %get-tuple-element.99) | copy-start | bytes 3145732
  319.0 10.6 %copy-start.40 = (f32[1,1,262144]{2,1,0:T(1,128)S(1)}, f32[1,1,262144]{2,1,0:T(1,128)}, u32[]{:S(2)}) copy-start(f32[1,1,262144]{2,1,0:T(1,128)} %get-tuple-element.100) | copy-start | bytes 3145732
  319.0 10.6 %copy-start.51 = (f32[1,262144]{1,0:T(1,128)S(1)}, f32[1,262144]{1,0:T(1,128)}, u32[]{:S(2)}) copy-start(f32[1,262144]{1,0:T(1,128)} %get-tuple-element.102) | copy-start | bytes 3145732
  319.0 10.6 %copy-start.52 = (f32[1,262144]{1,0:T(1,128)S(1)}, f32[1,262144]{1,0:T(1,128)}, u32[]{:S(2)}) copy-start(f32[1,262144]{1,0:T(1,128)} %get-tuple-element.104) | copy-start | bytes 3145732
  319.1 10.6 %copy-start.59 = (f32[262144]{0:T(1024)S(1)}, f32[262144]{0:T(1024)}, u32[]{:S(2)}) copy-start(f32[262144]{0:T(1024)} %param.5) | copy-start | bytes 3145732
  331.7 7.6 %copy-start.3 = (f32[262144]{0:T(1024)}, f32[262144]{0:T(1024)S(1)}, u32[]{:S(2)}) copy-start(f32[262144]{0:T(1024)S(1)} %get-tuple-element.93) | copy-start | bytes 3145732
  331.7 7.6 %copy-start.7 = (f32[262144]{0:T(1024)}, f32[262144]{0:T(1024)S(1)}, u32[]{:S(2)}) copy-start(f32[262144]{0:T(1024)S(1)} %get-tuple-element.94) | copy-start | bytes 3145732
  331.8 7.6 %copy-start.11 = (f32[262144]{0:T(1024)}, f32[262144]{0:T(1024)S(1)}, u32[]{:S(2)}) copy-start(f32[262144]{0:T(1024)S(1)} %get-tuple-element.132) | copy-start | bytes 3145732
  400.2 10.6 %copy-start.4 = (f32[262144]{0:T(1024)S(1)}, f32[262144]{0:T(1024)}, u32[]{:S(2)}) copy-start(f32[262144]{0:T(1024)} %copy-done.3) | copy-start | bytes 3145732
  400.2 10.6 %copy-start.8 = (f32[262144]{0:T(1024)S(1)}, f32[262144]{0:T(1024)}, u32[]{:S(2)}) copy-start(f32[262144]{0:T(1024)} %copy-done.7) | copy-start | bytes 3145732
  400.2 10.6 %copy-start.12 = (f32[262144]{0:T(1024)S(1)}, f32[262144]{0:T(1024)}, u32[]{:S(2)}) copy-start(f32[262144]{0:T(1024)} %copy-done.11) | copy-start | bytes 3145732
  481.0 10.6 %copy-start.5 = (f32[262144]{0:T(1024)S(1)}, f32[262144]{0:T(1024)}, u32[]{:S(2)}) copy-start(f32[262144]{0:T(1024)} %copy-done.3) | copy-start | bytes 3145732
  481.0 10.6 %copy-start.9 = (f32[262144]{0:T(1024)S(1)}, f32[262144]{0:T(1024)}, u32[]{:S(2)}) copy-start(f32[262144]{0:T(1024)} %copy-done.7) | copy-start | bytes 3145732
  481.0 10.6 %copy-start.13 = (f32[262144]{0:T(1024)S(1)}, f32[262144]{0:T(1024)}, u32[]{:S(2)}) copy-start(f32[262144]{0:T(1024)} %copy-done.11) | copy-start | bytes 3145732
  481.1 10.6 %copy-start.32 = (f32[1,1,262144]{2,1,0:T(1,128)S(1)}, f32[1,1,262144]{2,1,0:T(1,128)}, u32[]{:S(2)}) copy-start(f32[1,1,262144]{2,1,0:T(1,128)} %copy-done.31) | copy-start | bytes 3145732
  481.1 10.6 %copy-start.34 = (f32[1,1,262144]{2,1,0:T(1,128)S(1)}, f32[1,1,262144]{2,1,0:T(1,128)}, u32[]{:S(2)}) copy-start(f32[1,1,262144]{2,1,0:T(1,128)} %copy-done.33) | copy-start | bytes 3145732
  481.1 10.6 %copy-start.36 = (f32[1,1,262144]{2,1,0:T(1,128)S(1)}, f32[1,1,262144]{2,1,0:T(1,128)}, u32[]{:S(2)}) copy-start(f32[1,1,262144]{2,1,0:T(1,128)} %copy-done.35) | copy-start | bytes 3145732
  481.1 10.6 %copy-start.38 = (f32[1,1,262144]{2,1,0:T(1,128)S(1)}, f32[1,1,262144]{2,1,0:T(1,128)}, u32[]{:S(2)}) copy-start(f32[1,1,262144]{2,1,0:T(1,128)} %copy-done.37) | copy-start | bytes 3145732
  493.2 5.9 copy-start.21
  567.8 11.6 %copy-start.16 = (f32[262144]{0:T(1024)S(1)}, f32[262144]{0:T(1024)}, u32[]{:S(2)}) copy-start(f32[262144]{0:T(1024)} %copy-done.15) | copy-start | bytes 3145732
  567.8 11.6 %copy-start.18 = (f32[262144]{0:T(1024)S(1)}, f32[262144]{0:T(1024)}, u32[]{:S(2)}) copy-start(f32[262144]{0:T(1024)} %copy-done.17) | copy-start | bytes 3145732
  567.8 11.6 %copy-start.20 = (f32[262144]{0:T(1024)S(1)}, f32[262144]{0:T(1024)}, u32[]{:S(2)}) copy-start(f32[262144]{0:T(1024)} %copy-done.19) | copy-start | bytes 3145732
  567.8 11.6 %copy-start.22 = (f32[262144]{0:T(1024)S(1)}, f32[262144]{0:T(1024)}, u32[]{:S(2)}) copy-start(f32[262144]{0:T(1024)} %copy-done.21) | copy-start | bytes 3145732
  584.0 16.1 %copy-start.53 = (f32[1,64,4096]{2,1,0:T(8,128)S(1)}, f32[1,64,4096]{2,1,0:T(8,128)}, u32[]{:S(2)}) copy-start(f32[1,64,4096]{2,1,0:T(8,128)} %stack.101) | copy-start | bytes 3145732
  584.0 16.1 %copy-start.54 = (f32[1,64,4096]{2,1,0:T(8,128)S(1)}, f32[1,64,4096]{2,1,0:T(8,128)}, u32[]{:S(2)}) copy-start(f32[1,64,4096]{2,1,0:T(8,128)} %stack.100) | copy-start | bytes 3145732
  584.0 16.1 %copy-start.55 = (f32[1,64,4096]{2,1,0:T(8,128)S(1)}, f32[1,64,4096]{2,1,0:T(8,128)}, u32[]{:S(2)}) copy-start(f32[1,64,4096]{2,1,0:T(8,128)} %stack.99) | copy-start | bytes 3145732
  (29 other events, 82.3 us)
Sparse Core Ops, SparseCore 0:
  25.1 157.3 all-reduce.1
where the time goes:
time: 616 us; the launch traced here: 608 us
  other arithmetic  209 us (34%)
  local copies, waits for them, and re-layouts  190 us (31%)
  waiting for transfers between devices  126 us (20%)
  matrix products  68.9 us (11%)
  between operations  15.4 us (2%)
    add x4, other arithmetic, hamiltonian(): single = -kinetic_coef * laplace + mean_field * state  152 us
    psum x1, waiting for transfers between devices, local(): summed = lax.psum(partial_value, ('grp', 'wf'))  126 us
    dot_general x22, matrix products, apply(): return jnp.dot(values, matrix, precision=lax.Precision.HIGHEST)  68.9 us
    slice x3, local copies, waits for them, and re-layouts, hamiltonian(): single[..., 1, :] + pair_real * state[..., 3, :]  32.6 us
    slice x8, local copies, waits for them, and re-layouts, neighbour_sum(): jnp.roll(field, -(grid - 1) * grid, -1)  21.8 us
    slice x1, local copies, waits for them, and re-layouts, local(): summed[2]  20.7 us
    slice x8, local copies, waits for them, and re-layouts, neighbour_sum(): jnp.roll(field, 1, -1)  19.7 us
    slice x8, local copies, waits for them, and re-layouts, neighbour_sum(): jnp.roll(field, 1 - grid, -1)  18.4 us
  transfers between devices with their start and end apart: 1, of which 1 were waited for; matrix products, arithmetic and copies ran while one was open for 5% of the time, Pallas kernels for 0%

commit v1 on v0

v1 whole, which is shorter than its diff:
```python
import math

import jax
import jax.numpy as jnp
import numpy as np
from jax import lax
from jax.experimental import pallas as pl
from jax.experimental.pallas import tpu as pltpu
from jax.sharding import PartitionSpec as P

MESH = pl.DeviceIdType.MESH
N = 64
ROWS = 2048
HALF = 1024
PITCH = 40
PADDED = N * PITCH + 8
GROUP = 8
time_step = 0.2
f32 = jnp.float32
bf16 = jnp.bfloat16

FLOWS = [(0, 0, "xyz"), (0, 1, "yzx"), (1, 0, "zxy"), (1, 1, "xyz"), (2, 0, "yzx"), (2, 1, "zxy")]
PARTS = (128, 32, 8)


def high_low(values):
    high = values.astype(bf16)
    return high, (values - high.astype(f32)).astype(bf16)


def tables():
    index = np.arange(N)
    angle = 2 * math.pi / N * (index[:, None] * index[None, :] % N)
    hartley = (np.cos(angle) + np.sin(angle)) / math.sqrt(N)
    symbol = 2 - 2 * np.cos(2 * math.pi / N * index)
    squared = symbol[:, None, None] + symbol[None, :, None] + symbol[None, None, :]
    spectral = np.where(squared > 0.001, 4 * math.pi * 0.25 / np.maximum(squared, 0.001), 0.0)
    spectral = spectral.reshape(ROWS, 128).astype(np.float32)

    def cut(matrix):
        high = matrix.astype(np.float32).astype(jnp.bfloat16)
        return high, (matrix - high.astype(np.float64)).astype(np.float32).astype(jnp.bfloat16)

    high, low = cut(hartley)
    first = np.concatenate([high, high, low], axis=1)
    blocks = [hartley[p::2, q::2] for p in range(2) for q in range(2)]
    high, low = cut(np.concatenate(blocks, axis=0))
    second = np.concatenate([high, high, low], axis=1)
    third = np.kron(np.eye(2), np.concatenate([hartley, hartley], axis=0))
    third = np.concatenate(cut(third), axis=0)
    lane = np.arange(128)
    near = np.zeros((128, 128), np.float32)
    near[(lane & 64) | ((lane + 1) & 63), lane] += 1
    near[(lane & 64) | ((lane + 63) & 63), lane] += 1
    near = np.concatenate([near, near], axis=0).astype(jnp.bfloat16)
    return first, second, third, spectral, near


def reduce_kernel(q_hbm, full, raw, part, met, got1, got2, got3, in_sem, send_sem, recv_sem):
    grp, wf = lax.axis_index("grp"), lax.axis_index("wf")
    core = grp % 2
    place = {"x": wf // 8, "y": wf % 4, "z": (wf // 4 % 2) * 2 + grp // 2}

    def device(axis, shift):
        at = dict(place)
        at[axis] = (place[axis] + shift) % 4
        return (at["z"] % 2 * 2 + core, at["x"] * 8 + at["z"] // 2 * 4 + at["y"])

    twin = (grp // 2 * 2 + 1 - core, wf)
    chunk = HALF // 2 * 4

    def load(part_index):
        half, side = part_index // 2, part_index % 2
        start = half * 2 * chunk + jnp.where(core == side, chunk, 0)
        rows = pl.ds(pl.multiple_of(start, 8), chunk)
        return pltpu.make_async_copy(q_hbm.at[rows], raw.at[rows], in_sem.at[part_index])

    for index in range(4):
        load(index).start()
    barrier = pltpu.get_barrier_semaphore()
    partners = [twin] + [device(axis, shift) for axis in "xyz" for shift in (1, 2, 3)]
    for partner in partners:
        pl.semaphore_signal(barrier, inc=1, device_id=partner, device_id_type=MESH)

    def send(flow, stage, source, target, to):
        pltpu.make_async_remote_copy(
            src_ref=source, dst_ref=target, send_sem=send_sem.at[flow, stage],
            recv_sem=recv_sem.at[flow, stage], device_id=to, device_id_type=MESH,
        ).start()

    def arrived(flow, stage, rows):
        ref = part.at[0, pl.ds(0, rows)]
        pltpu.make_async_remote_copy(
            src_ref=ref, dst_ref=ref, send_sem=send_sem.at[flow, stage],
            recv_sem=recv_sem.at[flow, stage], device_id=twin, device_id_type=MESH,
        ).wait_recv()

    def sent(flow, stage, rows):
        ref = part.at[0, pl.ds(0, rows)]
        pltpu.make_async_remote_copy(
            src_ref=ref, dst_ref=ref, send_sem=send_sem.at[flow, stage],
            recv_sem=recv_sem.at[flow, stage], device_id=twin, device_id_type=MESH,
        ).wait_send()

    def own(flow, depth):
        field, half, order = FLOWS[flow]
        start = half * HALF + core * 512
        for level in range(depth):
            start = start + place[order[level]] * PARTS[level]
        return start

    for index in range(4):
        half, side = index // 2, index % 2
        load(index).wait()
        begin = half * HALF + jnp.where(core == side, 512, 0)

        @pl.loop(0, 16)
        def partial(step):
            for sub in range(4):
                row = pl.multiple_of(begin + step * 32 + sub * 8, 8)
                a, b, c, d = (raw[pl.ds(row * 4 + k, 8, stride=4), :] for k in range(4))
                part[0, pl.ds(row, 8), :] = c * c + d * d
                part[1, pl.ds(row, 8), :] = a * c + b * d
                part[2, pl.ds(row, 8), :] = b * c - a * d

        if index == 0:
            pl.semaphore_wait(barrier, len(partners))
        if side == 0:
            for flow, (field, flow_half, _) in enumerate(FLOWS):
                if flow_half == half:
                    rows = pl.ds(pl.multiple_of(begin, 8), 512)
                    send(flow, 0, part.at[field, rows], met.at[flow], twin)

    def add_core(flow):
        field = FLOWS[flow][0]
        start = own(flow, 0)
        arrived(flow, 0, 512)

        @pl.loop(0, 8)
        def add(step):
            rows = pl.ds(pl.multiple_of(start + step * 64, 8), 64)
            part[field, rows, :] = part[field, rows, :] + met[flow, pl.ds(step * 64, 64), :]

        scatter(flow, 0)

    def scatter(flow, level):
        field, _, order = FLOWS[flow]
        size = PARTS[level]
        got = (got1, got2, got3)[level]
        for shift in (2, 1, 3):
            peer = (place[order[level]] + shift) % 4
            rows = pl.ds(pl.multiple_of(own(flow, level) + peer * size, 8), size)
            send(flow, 1 + level, part.at[field, rows],
                 got.at[flow, pl.ds((3 - shift) * size, size)], device(order[level], shift))

    def add_axis(flow, level):
        field = FLOWS[flow][0]
        size = PARTS[level]
        got = (got1, got2, got3)[level]
        start = pl.multiple_of(own(flow, level + 1), 8)
        arrived(flow, 1 + level, 3 * size)
        rows = pl.ds(start, size)
        total = part[field, rows, :]
        for slot in range(3):
            total = total + got[flow, pl.ds(slot * size, size), :]
        if level < 2:
            part[field, rows, :] = total
            scatter(flow, level + 1)
        else:
            full[field, rows, :] = total * (1.0 / 128.0)
            spread(flow, 2)

    def spread(flow, level):
        field, _, order = FLOWS[flow]
        rows = pl.ds(pl.multiple_of(own(flow, level + 1), 8), PARTS[level])
        for shift in (2, 1, 3):
            send(flow, 6 - level, full.at[field, rows], full.at[field, rows],
                 device(order[level], shift))

    def gathered(flow, level):
        arrived(flow, 6 - level, 3 * PARTS[level])
        if level > 0:
            spread(flow, level - 1)
        else:
            field = FLOWS[flow][0]
            rows = pl.ds(pl.multiple_of(own(flow, 0), 8), 512)
            send(flow, 7, full.at[field, rows], full.at[field, rows], twin)

    first, rest = (0, 1), (2, 3, 4, 5)

    def each(flows, call, *levels):
        for flow in flows:
            call(flow, *levels)

    each(first, add_core)
    each(rest, add_core)
    each(first, add_axis, 0)
    each(first, add_axis, 1)
    each(rest, add_axis, 0)
    each(first, add_axis, 2)
    each(rest, add_axis, 1)
    each(first, gathered, 2)
    each(rest, add_axis, 2)
    each(first, gathered, 1)
    each(rest, gathered, 2)
    each(first, gathered, 0)
    each(rest, gathered, 1)
    each(rest, gathered, 0)
    each(first + rest, lambda flow: arrived(flow, 7, 512))
    for flow in first + rest:
        for stage, rows in enumerate((512, 384, 96, 24, 24, 96, 384, 512)):
            sent(flow, stage, rows)


def evolve_kernel(q_hbm, sums_hbm, outer_hbm, coupling_hbm, first, second, third, spectral, near,
                  out_hbm, potentials, raw, sums, outer, coupling, work, hill, fields,
                  start, ping, pong, beside, in_sem, field_sem, out_sem):
    chunks = 8
    size = 8192 // chunks
    copies = [pltpu.make_async_copy(sums_hbm.at[field], sums.at[field], field_sem.at[field]) for field in range(3)]
    copies.append(pltpu.make_async_copy(outer_hbm, outer, field_sem.at[3]))
    copies.append(pltpu.make_async_copy(coupling_hbm, coupling, field_sem.at[4]))
    for copy in copies:
        copy.start()

    def load(index):
        rows = pl.ds(index * size, size)
        return pltpu.make_async_copy(q_hbm.at[rows], raw.at[rows], in_sem.at[index])

    def save(index):
        rows = pl.ds(index * size, size)
        return pltpu.make_async_copy(raw.at[rows], out_hbm.at[rows], out_sem.at[index])

    for index in range(chunks):
        load(index).start()

    def thrice(values):
        high, low = high_low(values)
        return jnp.concatenate([high, low, high], axis=0)

    def along_first(source, target):
        @pl.loop(0, 8)
        def columns(step):
            slices = [pl.ds(step * 4 + k, N, stride=32) for k in range(4)]
            values = jnp.concatenate([source[s, :] for s in slices], axis=1)
            result = jnp.dot(first[...], thrice(values), preferred_element_type=f32)
            for k in range(4):
                target[slices[k], :] = result[:, 128 * k:128 * k + 128]

    def along_rest(source, target, weigh):
        low_lanes = lax.broadcasted_iota(jnp.int32, (32, 128), 1) < 64

        @pl.loop(0, 8)
        def planes(step):
            base = pl.multiple_of(step * 256, 256)
            values = jnp.concatenate([source[pl.ds(base + 32 * k, 32), :] for k in range(8)], axis=1)
            mixed = jnp.dot(second[...], thrice(values), preferred_element_type=f32)
            parts = []
            for k in range(8):
                piece = mixed[:, 128 * k:128 * k + 128]
                parts.append(jnp.concatenate([
                    jnp.where(low_lanes, piece[0:32], piece[32:64]),
                    jnp.where(low_lanes, piece[64:96], piece[96:128])], axis=1))
            high, low = high_low(jnp.concatenate(parts, axis=0))
            result = jnp.dot(high, third[0:256, :], preferred_element_type=f32)
            result = result + jnp.dot(low, third[0:256, :], preferred_element_type=f32)
            result = result + jnp.dot(high, third[256:512, :], preferred_element_type=f32)
            if weigh:
                result = result * spectral[pl.ds(base, 256), :]
            target[pl.ds(base, 256), :] = result

    copies[0].wait()
    along_first(sums.at[0], work)
    along_rest(work, hill, True)
    along_rest(hill, work, False)
    along_first(work, hill)

    def put(state, component, plane, block, values):
        base = plane * PITCH + 8
        state[component, pl.ds(base + 8 * block, 8), :] = values
        if block == 0:
            state[component, pl.ds(base + 32, 1), :] = values[0:1]
        if block == 3:
            state[component, pl.ds(base - 1, 1), :] = values[7:8]

    for index in range(chunks):
        load(index).wait()

        @pl.loop(index * (N // chunks), (index + 1) * (N // chunks))
        def planes(plane):
            for component in range(4):
                for block in range(4):
                    put(start, component, plane, block,
                        raw[pl.ds(plane * 128 + block * 32 + component, 8, stride=4), :])

    for copy in copies[1:]:
        copy.wait()

    @pl.loop(0, 64)
    def fill(step):
        for sub in range(4):
            rows = pl.ds(pl.multiple_of(step * 32 + sub * 8, 8), 8)
            mean = outer[rows, :] + sums[0, rows, :] + hill[rows, :]
            scale = -2.0 * coupling[rows, :]
            fields[0, rows, :] = 2.0 * mean + 6.0
            fields[1, rows, :] = scale * sums[1, rows, :]
            fields[2, rows, :] = scale * sums[2, rows, :]

    held = pl.ds(lax.axis_index("grp") * 512 + lax.axis_index("wf"), 16, stride=32)
    potentials[0] = outer[held, :] + sums[0, held, :] + hill[held, :]
    potentials[1] = -coupling[held, :] * sums[1, held, :]
    potentials[2] = -coupling[held, :] * sums[2, held, :]

    upper = lax.broadcasted_iota(jnp.int32, (8, 128), 1) >= 64

    def step(source, factor, store):
        def group(index):
            plane0 = index * GROUP
            lines = []
            for sub in range(GROUP):
                for component in range(4):
                    values = source[component, pl.ds((plane0 + sub) * PITCH + 8, 32), :]
                    lines.append(jnp.concatenate(high_low(values), axis=1))
            beside[...] = jnp.dot(jnp.concatenate(lines, axis=0), near[...], preferred_element_type=f32)
            for sub in range(GROUP):
                plane = plane0 + sub
                base = plane * PITCH + 8
                before = lax.rem(plane + N - 1, N) * PITCH + 8
                after = lax.rem(plane + 1, N) * PITCH + 8
                for block in range(4):
                    row = 8 * block
                    state, total = [], []
                    for component in range(4):
                        here = source[component, pl.ds(base + row, 8), :]
                        up = source[component, pl.ds(base + row - 1, 8), :]
                        down = source[component, pl.ds(base + row + 1, 8), :]
                        across = pltpu.roll(here + jnp.where(upper, up, down), 64, 1)
                        along = source[component, pl.ds(before + row, 8), :] + source[component, pl.ds(after + row, 8), :]
                        total.append(beside[pl.ds((sub * 4 + component) * 32 + row, 8), :] + along + across)
                        state.append(here)
                    rows = pl.ds(pl.multiple_of(plane * 32, 32) + row, 8)
                    mean, real, imag = fields[0, rows, :], fields[1, rows, :], fields[2, rows, :]
                    a, b, c, d = state
                    made = [mean * a - total[0] + (real * c - imag * d),
                            mean * b - total[1] + (real * d + imag * c),
                            (real * a + imag * b) - (mean * c - total[2]),
                            (real * b - imag * a) - (mean * d - total[3])]
                    old = [start[component, pl.ds(base + row, 8), :] for component in range(4)]
                    half = 0.5 * factor
                    store(plane, block, [old[0] + half * made[1], old[1] - half * made[0],
                                         old[2] + half * made[3], old[3] - half * made[2]])
        return group

    def into(state):
        def store(plane, block, values):
            for component in range(4):
                put(state, component, plane, block, values[component])
        return store

    def finish(plane, block, values):
        for component in range(4):
            raw[pl.ds(plane * 128 + block * 32 + component, 8, stride=4), :] = values[component]

    for source, degree, target in ((start, 4, ping), (ping, 3, pong), (pong, 2, ping)):
        pl.loop(0, N // GROUP)(step(source, time_step / degree, into(target)))
    last = step(ping, time_step, finish)

    @pl.loop(0, chunks)
    def groups(index):
        last(index)
        save(index).start()

    for index in range(chunks):
        save(index).wait()


def local(quasi, outer_field, coupling):
    rows = quasi.reshape(4, ROWS, 128).transpose(1, 0, 2).reshape(4 * ROWS, 128)
    anywhere = pl.BlockSpec(memory_space=pl.ANY)
    inside = pl.BlockSpec(memory_space=pltpu.VMEM)
    sums = pl.pallas_call(
        reduce_kernel,
        out_shape=jax.ShapeDtypeStruct((3, ROWS, 128), f32),
        in_specs=[anywhere],
        out_specs=inside,
        scratch_shapes=[
            pltpu.VMEM((4 * ROWS, 128), f32),
            pltpu.VMEM((3, ROWS, 128), f32),
            pltpu.VMEM((6, 512, 128), f32),
            pltpu.VMEM((6, 384, 128), f32),
            pltpu.VMEM((6, 96, 128), f32),
            pltpu.VMEM((6, 24, 128), f32),
            pltpu.SemaphoreType.DMA((4,)),
            pltpu.SemaphoreType.DMA((6, 8)),
            pltpu.SemaphoreType.DMA((6, 8)),
        ],
        compiler_params=pltpu.CompilerParams(
            collective_id=0, has_side_effects=True, vmem_limit_bytes=40 * 2**20),
        name="reduce",
    )(rows)
    weights = tables()
    evolved, potentials = pl.pallas_call(
        evolve_kernel,
        out_shape=(jax.ShapeDtypeStruct((4 * ROWS, 128), f32), jax.ShapeDtypeStruct((3, 16, 128), f32)),
        in_specs=[anywhere] * 4 + [inside] * 5,
        out_specs=(anywhere, inside),
        scratch_shapes=[
            pltpu.VMEM((4 * ROWS, 128), f32),
            pltpu.VMEM((3, ROWS, 128), f32),
            pltpu.VMEM((ROWS, 128), f32),
            pltpu.VMEM((ROWS, 128), f32),
            pltpu.VMEM((ROWS, 128), f32),
            pltpu.VMEM((ROWS, 128), f32),
            pltpu.VMEM((3, ROWS, 128), f32),
            pltpu.VMEM((4, PADDED, 128), f32),
            pltpu.VMEM((4, PADDED, 128), f32),
            pltpu.VMEM((4, PADDED, 128), f32),
            pltpu.VMEM((GROUP * 128, 128), f32),
            pltpu.SemaphoreType.DMA((8,)),
            pltpu.SemaphoreType.DMA((5,)),
            pltpu.SemaphoreType.DMA((8,)),
        ],
        compiler_params=pltpu.CompilerParams(vmem_limit_bytes=56 * 2**20),
        name="evolve",
    )(rows, sums, outer_field.reshape(ROWS, 128), coupling.reshape(ROWS, 128), *[jnp.asarray(w) for w in weights])
    evolved = evolved.reshape(ROWS, 4, 128).transpose(1, 0, 2).reshape(1, 4, ROWS * 128)
    return evolved, potentials


def solution(mesh):
    return jax.shard_map(
        local,
        mesh=mesh,
        in_specs=(P(("grp", "wf"), None, None), P(), P()),
        out_specs=(P(("grp", "wf"), None, None), P(None, "grp", "wf")),
        check_vma=False,
    )
```

time: 616 us -> 78.7 us (0.13); the launches traced: 608 us -> 78.5 us
  other arithmetic: 209 us -> 0 us
  local copies, waits for them, and re-layouts: 190 us -> 3.83 us
  waiting for transfers between devices: 126 us -> 0 us
  Pallas kernels: 0 us -> 74 us
  matrix products: 68.9 us -> 0 us
  between operations: 15.4 us -> 0.65 us
    add x7 -> x0, other arithmetic: 172 us -> none  [the longest x4 152 us: hamiltonian(): single = -kinetic_coef * laplace + mean_field * state]
    slice x45 -> x0, local copies, waits for them, and re-layouts: 160 us -> none  [the longest x3 32.6 us: hamiltonian(): single[..., 1, :] + pair_real * state[..., 3, :]]
    psum x1 -> x0, waiting for transfers between devices: 126 us -> none  [local(): summed = lax.psum(partial_value, ('grp', 'wf'))]
    pallas_call x0 -> x2, Pallas kernels: none -> 74 us  [the longest x1 43.4 us: local(): pl.pallas_call(reduce_kernel, out_shape=jax.ShapeDtypeStruct((3, ROWS, 12...]
    dot_general x22 -> x0, matrix products: 68.9 us -> none  [apply(): return jnp.dot(values, matrix, precision=lax.Precision.HIGHEST)]
    slice x1 -> x0, other arithmetic: 13.3 us -> none  [local(): quasi[:, 0] * quasi[:, 2] + quasi[:, 1] * quasi[:, 3]]
    another operation x4 -> x0, other arithmetic: 12.8 us -> none  [the longest x3 12.2 us: propagate(): jnp.stack([factor * applied[..., 1, :], -factor * applied[..., 0, :], fac...]
    div x2 -> x0, local copies, waits for them, and re-layouts: 6.82 us -> none  [the longest x1 3.5 us: transform(): new_imag = (apply(cosine, moved_imag) + apply(sine, moved_real)) / length]
  transfers between devices with their start and end apart: 1 -> 0, of which waited for: 1 -> 0; matrix products, arithmetic and copies ran while one was open for 5% -> 0% of each run, Pallas kernels for 0% -> 0%
where the time goes in v1:
time: 78.7 us; the launch traced here: 78.5 us
  Pallas kernels  74 us (94%)
  local copies, waits for them, and re-layouts  3.83 us (5%)
    pallas_call x1, Pallas kernels, local(): pl.pallas_call(reduce_kernel, out_shape=jax.ShapeDtypeStruct((3, ROWS, 12...  43.4 us
    pallas_call x1, Pallas kernels, local(): pl.pallas_call(evolve_kernel, out_shape=(jax.ShapeDtypeStruct((4 * ROWS,...  30.7 us
    unnamed x4, local copies, waits for them, and re-layouts  3.83 us

profile of v1, /device:TPU:1, one launch (start us, length us, event | category | flops | bytes accessed | tf_op | source)
XLA Modules:
  0.0 78.5 jit_solution(16263833090680392108)
XLA Ops:
  0.6 0.0 copy-start
  0.6 2.2 %copy-done = f32[1,4,262144]{2,1,0:T(4,128)S(1)} copy-done((f32[1,4,262144]{2,1,0:T(4,128)S(1)}, f32[1,4,262144]{2,1,0:T(4,128)}, u32[]{:S(2)}) %copy-start) | copy-done | bytes 4194328
  2.8 43.4 %reduce.1.sums_hbm = f32[3,2048,128]{2,1,0:T(8,128)S(1)} custom-call(f32[8192,128]{1,0:T(8,128)S(1)} %bitcast.13), custom_call_target="tpu_custom_call" | custom-call | tf_op jit(solution)/shard_map/reduce/pallas_call | solution.py:381
  46.2 0.0 copy-start.1
  46.2 1.6 %copy-done.1 = f32[3,2048,128]{2,1,0:T(8,128)} copy-done((f32[3,2048,128]{2,1,0:T(8,128)}, f32[3,2048,128]{2,1,0:T(8,128)S(1)}, u32[]{:S(2)}) %copy-start.1) | copy-done | bytes 3145752
  47.9 30.7 %evolve.1 = (f32[8192,128]{1,0:T(8,128)}, f32[3,16,128]{2,1,0:T(8,128)}) custom-call(f32[8192,128]{1,0:T(8,128)} %bitcast.12, f32[3,2048,128]{2,1,0:T(8,128)} %copy-done.1, f32[2048,128]{1,0:T(8,128)} %bitcast.14, f32[2048,128]{1,0:T(8,128)} %bitcast.15, bf16[64,192]{1,0:T(8,128)(2,1)} %constant.10.clone.first, bf16[128,96]{1,0:T(8,128)(2,1)} %constant.11.clone.second, ...), custom_call_target="tpu_custom_call" | custom-call | tf_op jit(solution)/shard_map/evolve/pallas_call | solution.py:402
Async XLA Ops:
  0.6 2.2 %copy-start = (f32[1,4,262144]{2,1,0:T(4,128)S(1)}, f32[1,4,262144]{2,1,0:T(4,128)}, u32[]{:S(2)}) copy-start(f32[1,4,262144]{2,1,0:T(4,128)} %param.8) | copy-start | bytes 12582916
  46.2 1.7 %copy-start.1 = (f32[3,2048,128]{2,1,0:T(8,128)}, f32[3,2048,128]{2,1,0:T(8,128)S(1)}, u32[]{:S(2)}) copy-start(f32[3,2048,128]{2,1,0:T(8,128)S(1)} %reduce.1.sums_hbm) | copy-start | bytes 9437188

commit v2 on v1

v2 whole, which is shorter than its diff:
```python
import math

import jax
import jax.numpy as jnp
import numpy as np
from jax import lax
from jax.experimental import pallas as pl
from jax.experimental.pallas import tpu as pltpu
from jax.sharding import PartitionSpec as P

MESH = pl.DeviceIdType.MESH
N = 64
ROWS = 2048
HALF = 1024
PITCH = 40
PADDED = N * PITCH + 8
GROUP = 8
VMEM_MIB = 58
time_step = 0.2
f32 = jnp.float32
bf16 = jnp.bfloat16

FLOWS = [(0, 0, "xyz"), (0, 1, "yzx"), (1, 0, "zxy"), (1, 1, "xyz"), (2, 0, "yzx"), (2, 1, "zxy")]
PARTS = (128, 32, 8)


def high_low(values):
    high = values.astype(bf16)
    return high, (values - high.astype(f32)).astype(bf16)


def tables():
    index = np.arange(N)
    angle = 2 * math.pi / N * (index[:, None] * index[None, :] % N)
    hartley = (np.cos(angle) + np.sin(angle)) / math.sqrt(N)
    symbol = 2 - 2 * np.cos(2 * math.pi / N * index)
    squared = symbol[:, None, None] + symbol[None, :, None] + symbol[None, None, :]
    spectral = np.where(squared > 0.001, 4 * math.pi * 0.25 / np.maximum(squared, 0.001), 0.0)
    spectral = spectral.reshape(ROWS, 128).astype(np.float32)

    def cut(matrix):
        high = matrix.astype(np.float32).astype(jnp.bfloat16)
        return high, (matrix - high.astype(np.float64)).astype(np.float32).astype(jnp.bfloat16)

    high, low = cut(hartley)
    first = np.concatenate([high, high, low], axis=1)
    blocks = [hartley[p::2, q::2] for p in range(2) for q in range(2)]
    high, low = cut(np.concatenate(blocks, axis=0))
    second = np.concatenate([high, high, low], axis=1)
    third = np.kron(np.eye(2), np.concatenate([hartley, hartley], axis=0))
    third = np.concatenate(cut(third), axis=0)
    lane = np.arange(128)
    near = np.zeros((128, 128), np.float32)
    near[(lane & 64) | ((lane + 1) & 63), lane] += 1
    near[(lane & 64) | ((lane + 63) & 63), lane] += 1
    near = np.concatenate([near, near], axis=0).astype(jnp.bfloat16)
    return first, second, third, spectral, near


def put(state, component, plane, block, values):
    base = plane * PITCH + 8
    state[component, pl.ds(base + 8 * block, 8), :] = values
    if block == 0:
        state[component, pl.ds(base + 32, 1), :] = values[0:1]
    if block == 3:
        state[component, pl.ds(base - 1, 1), :] = values[7:8]


def beside_planes(source, near, beside, plane0):
    lines = []
    for sub in range(GROUP):
        for component in range(4):
            values = source[component, pl.ds((plane0 + sub) * PITCH + 8, 32), :]
            lines.append(jnp.concatenate(high_low(values), axis=1))
    beside[...] = jnp.dot(jnp.concatenate(lines, axis=0), near[...], preferred_element_type=f32)


def neighbours(source, beside, upper, plane, sub, component, row):
    base = plane * PITCH + 8
    before = lax.rem(plane + N - 1, N) * PITCH + 8
    after = lax.rem(plane + 1, N) * PITCH + 8
    here = source[component, pl.ds(base + row, 8), :]
    up = source[component, pl.ds(base + row - 1, 8), :]
    down = source[component, pl.ds(base + row + 1, 8), :]
    across = pltpu.roll(here + jnp.where(upper, up, down), 64, 1)
    along = source[component, pl.ds(before + row, 8), :] + source[component, pl.ds(after + row, 8), :]
    return here, beside[pl.ds((sub * 4 + component) * 32 + row, 8), :] + along + across


def kernel(q_hbm, outer_hbm, coupling_hbm, first_hbm, second_hbm, third_hbm, spectral_hbm, near_hbm,
           out_hbm, potentials, raw, fields, start, laplace, ping, pong, part, full, met, got1, got2, got3,
           outer, coupling, first, second, third, spectral, near, work, hill, beside,
           in_sem, send_sem, recv_sem, side_sem, out_sem):
    grp, wf = lax.axis_index("grp"), lax.axis_index("wf")
    core = grp % 2
    place = {"x": wf // 8, "y": wf % 4, "z": (wf // 4 % 2) * 2 + grp // 2}

    def device(axis, shift):
        at = dict(place)
        at[axis] = (place[axis] + shift) % 4
        return (at["z"] % 2 * 2 + core, at["x"] * 8 + at["z"] // 2 * 4 + at["y"])

    twin = (grp // 2 * 2 + 1 - core, wf)
    pieces = ((0, 0), (1, 0), (0, 1), (1, 1))

    def begin_of(piece):
        half, side = pieces[piece]
        return half * HALF + jnp.where(core == side, 512, 0)

    def load(piece):
        rows = pl.ds(pl.multiple_of(begin_of(piece) * 4, 8), 2048)
        return pltpu.make_async_copy(q_hbm.at[rows], raw.at[rows], in_sem.at[piece])

    for piece in range(4):
        load(piece).start()
    barrier = pltpu.get_barrier_semaphore()
    partners = [twin] + [device(axis, shift) for axis in "xyz" for shift in (1, 2, 3)]
    for partner in partners:
        pl.semaphore_signal(barrier, inc=1, device_id=partner, device_id_type=MESH)
    tables_in = [
        pltpu.make_async_copy(source, target, side_sem.at[index])
        for index, (source, target) in enumerate((
            (near_hbm, near), (first_hbm, first), (second_hbm, second), (third_hbm, third),
            (spectral_hbm, spectral), (outer_hbm, outer), (coupling_hbm, coupling)))
    ]
    for copy in tables_in:
        copy.start()

    def send(flow, stage, source, target, to):
        pltpu.make_async_remote_copy(
            src_ref=source, dst_ref=target, send_sem=send_sem.at[flow, stage],
            recv_sem=recv_sem.at[flow, stage], device_id=to, device_id_type=MESH,
        ).start()

    def whole(flow, stage, rows):
        ref = part.at[0, pl.ds(0, rows)]
        return pltpu.make_async_remote_copy(
            src_ref=ref, dst_ref=ref, send_sem=send_sem.at[flow, stage],
            recv_sem=recv_sem.at[flow, stage], device_id=twin, device_id_type=MESH,
        )

    def arrived(flow, stage, rows):
        whole(flow, stage, rows).wait_recv()

    def own(flow, depth):
        field, half, order = FLOWS[flow]
        begin = half * HALF + core * 512
        for level in range(depth):
            begin = begin + place[order[level]] * PARTS[level]
        return begin

    def partial(piece):
        half, side = pieces[piece]
        begin = begin_of(piece)
        load(piece).wait()

        @pl.loop(0, 8)
        def rows_of(step):
            for sub in range(8):
                row = pl.multiple_of(begin + step * 64 + sub * 8, 8)
                a, b, c, d = (raw[pl.ds(row * 4 + k, 8, stride=4), :] for k in range(4))
                part[0, pl.ds(row, 8), :] = c * c + d * d
                part[1, pl.ds(row, 8), :] = a * c + b * d
                part[2, pl.ds(row, 8), :] = b * c - a * d

        if piece == 0:
            pl.semaphore_wait(barrier, len(partners))
        if side == 0:
            for flow, (field, flow_half, _) in enumerate(FLOWS):
                if flow_half == half:
                    rows = pl.ds(pl.multiple_of(begin, 8), 512)
                    send(flow, 0, part.at[field, rows], met.at[flow], twin)

    def add_core(flow):
        field = FLOWS[flow][0]
        begin = own(flow, 0)
        arrived(flow, 0, 512)

        @pl.loop(0, 4)
        def add(step):
            rows = pl.ds(pl.multiple_of(begin + step * 128, 8), 128)
            part[field, rows, :] = part[field, rows, :] + met[flow, pl.ds(step * 128, 128), :]

        scatter(flow, 0)

    def scatter(flow, level):
        field, _, order = FLOWS[flow]
        size = PARTS[level]
        got = (got1, got2, got3)[level]
        for shift in (2, 1, 3):
            peer = (place[order[level]] + shift) % 4
            rows = pl.ds(pl.multiple_of(own(flow, level) + peer * size, 8), size)
            send(flow, 1 + level, part.at[field, rows],
                 got.at[flow, pl.ds((3 - shift) * size, size)], device(order[level], shift))

    def add_axis(flow, level):
        field = FLOWS[flow][0]
        size = PARTS[level]
        got = (got1, got2, got3)[level]
        begin = pl.multiple_of(own(flow, level + 1), 8)
        arrived(flow, 1 + level, 3 * size)
        rows = pl.ds(begin, size)
        total = part[field, rows, :]
        for slot in range(3):
            total = total + got[flow, pl.ds(slot * size, size), :]
        if level < 2:
            part[field, rows, :] = total
            scatter(flow, level + 1)
        else:
            full[field, rows, :] = total * (1.0 / 128.0)
            spread(flow, 2)

    def spread(flow, level):
        field, _, order = FLOWS[flow]
        rows = pl.ds(pl.multiple_of(own(flow, level + 1), 8), PARTS[level])
        for shift in (2, 1, 3):
            send(flow, 6 - level, full.at[field, rows], full.at[field, rows],
                 device(order[level], shift))

    def gathered(flow, level):
        arrived(flow, 6 - level, 3 * PARTS[level])
        if level > 0:
            spread(flow, level - 1)
        else:
            field = FLOWS[flow][0]
            rows = pl.ds(pl.multiple_of(own(flow, 0), 8), 512)
            send(flow, 7, full.at[field, rows], full.at[field, rows], twin)

    def thrice(values):
        high, low = high_low(values)
        return jnp.concatenate([high, low, high], axis=0)

    def along_first(source, target, level):
        @pl.loop(0, 2)
        def columns(group):
            for sub in range(4):
                step = group * 4 + sub
                slices = [pl.ds(step * 4 + k, N, stride=32) for k in range(4)]
                values = jnp.concatenate([source[s, :] for s in slices], axis=1)
                if level is not None:
                    values = values - level
                result = jnp.dot(first[...], thrice(values), preferred_element_type=f32)
                for k in range(4):
                    target[slices[k], :] = result[:, 128 * k:128 * k + 128]

    def along_rest(source, target, weigh):
        low_lanes = lax.broadcasted_iota(jnp.int32, (32, 128), 1) < 64

        @pl.loop(0, 2)
        def planes(group):
            for sub in range(4):
                base = pl.multiple_of((group * 4 + sub) * 256, 256)
                values = jnp.concatenate([source[pl.ds(base + 32 * k, 32), :] for k in range(8)], axis=1)
                mixed = jnp.dot(second[...], thrice(values), preferred_element_type=f32)
                parts = []
                for k in range(8):
                    piece = mixed[:, 128 * k:128 * k + 128]
                    parts.append(jnp.concatenate([
                        jnp.where(low_lanes, piece[0:32], piece[32:64]),
                        jnp.where(low_lanes, piece[64:96], piece[96:128])], axis=1))
                high, low = high_low(jnp.concatenate(parts, axis=0))
                result = jnp.dot(high, third[0:256, :], preferred_element_type=f32)
                result = result + jnp.dot(low, third[0:256, :], preferred_element_type=f32)
                result = result + jnp.dot(high, third[256:512, :], preferred_element_type=f32)
                if weigh:
                    result = result * spectral[pl.ds(base, 256), :]
                target[pl.ds(base, 256), :] = result

    def prepare():
        @pl.loop(0, 32)
        def planes(pair):
            for plane in (pair * 2, pair * 2 + 1):
                for component in range(4):
                    for block in range(4):
                        put(start, component, plane, block,
                            raw[pl.ds(plane * 128 + block * 32 + component, 8, stride=4), :])

        tables_in[0].wait()
        upper = lax.broadcasted_iota(jnp.int32, (8, 128), 1) >= 64

        @pl.loop(0, N // GROUP)
        def groups(index):
            plane0 = index * GROUP
            beside_planes(start, near, beside, plane0)
            for sub in range(GROUP):
                plane = plane0 + sub
                for block in range(4):
                    rows = pl.ds(pl.multiple_of(plane * 32, 32) + 8 * block, 8)
                    for component in range(4):
                        laplace[component, rows, :] = neighbours(
                            start, beside, upper, plane, sub, component, 8 * block)[1]

    lead, rest = (0, 1), (2, 3, 4, 5)

    def each(flows, call, *levels):
        for flow in flows:
            call(flow, *levels)

    partial(0)
    partial(1)
    partial(2)
    add_core(0)
    partial(3)
    add_core(1)
    each(rest, add_core)
    prepare()
    each(lead, add_axis, 0)
    each(lead, add_axis, 1)
    each(rest, add_axis, 0)
    each(lead, add_axis, 2)
    each(rest, add_axis, 1)
    each(lead, gathered, 2)
    each(rest, add_axis, 2)
    each(lead, gathered, 1)
    each(rest, gathered, 2)
    each(lead, gathered, 0)
    each(rest, gathered, 1)
    for copy in tables_in[1:]:
        copy.wait()
    each(lead, lambda flow: arrived(flow, 7, 512))
    total = full[0, 0:64, :]
    for index in range(1, 32):
        total = total + full[0, 64 * index:64 * index + 64, :]
    along_first(full.at[0], work, jnp.sum(total) * (1.0 / (ROWS * 128)))
    along_rest(work, hill, True)
    each(rest, gathered, 0)
    along_rest(hill, work, False)
    along_first(work, hill, None)
    each(rest, lambda flow: arrived(flow, 7, 512))

    @pl.loop(0, 32)
    def fill(step):
        for sub in range(8):
            rows = pl.ds(pl.multiple_of(step * 64 + sub * 8, 8), 8)
            scale = -2.0 * coupling[rows, :]
            fields[0, rows, :] = 2.0 * (outer[rows, :] + full[0, rows, :] + hill[rows, :]) + 6.0
            fields[1, rows, :] = scale * full[1, rows, :]
            fields[2, rows, :] = scale * full[2, rows, :]

    held = pl.ds(lax.axis_index("grp") * 512 + lax.axis_index("wf"), 16, stride=32)
    potentials[0] = 0.5 * fields[0, held, :] - 3.0
    potentials[1] = 0.5 * fields[1, held, :]
    potentials[2] = 0.5 * fields[2, held, :]
    upper = lax.broadcasted_iota(jnp.int32, (8, 128), 1) >= 64

    def combine(plane, block, state, total, factor, store):
        rows = pl.ds(pl.multiple_of(plane * 32, 32) + 8 * block, 8)
        mean, real, imag = fields[0, rows, :], fields[1, rows, :], fields[2, rows, :]
        a, b, c, d = state
        made = [mean * a - total[0] + (real * c - imag * d),
                mean * b - total[1] + (real * d + imag * c),
                (real * a + imag * b) - (mean * c - total[2]),
                (real * b - imag * a) - (mean * d - total[3])]
        old = [start[component, pl.ds(plane * PITCH + 8 + 8 * block, 8), :] for component in range(4)]
        half = 0.5 * factor
        store(plane, block, [old[0] + half * made[1], old[1] - half * made[0],
                             old[2] + half * made[3], old[3] - half * made[2]])

    def step(source, factor, store):
        def group(index):
            plane0 = index * GROUP
            beside_planes(source, near, beside, plane0)
            for sub in range(GROUP):
                for block in range(4):
                    both = [neighbours(source, beside, upper, plane0 + sub, sub, component, 8 * block)
                            for component in range(4)]
                    combine(plane0 + sub, block, [b[0] for b in both], [b[1] for b in both], factor, store)
        return group

    def into(state):
        def store(plane, block, values):
            for component in range(4):
                put(state, component, plane, block, values[component])
        return store

    def finish(plane, block, values):
        for component in range(4):
            raw[pl.ds(plane * 128 + block * 32 + component, 8, stride=4), :] = values[component]

    @pl.loop(0, N // 4)
    def opening(index):
        for sub in range(4):
            plane = index * 4 + sub
            for block in range(4):
                rows = pl.ds(pl.multiple_of(plane * 32, 32) + 8 * block, 8)
                state = [start[component, pl.ds(plane * PITCH + 8 + 8 * block, 8), :] for component in range(4)]
                total = [laplace[component, rows, :] for component in range(4)]
                combine(plane, block, state, total, time_step / 4, into(ping))

    for source, degree, target in ((ping, 3, pong), (pong, 2, ping)):
        pl.loop(0, N // GROUP)(step(source, time_step / degree, into(target)))
    last = step(ping, time_step, finish)

    def save(index):
        rows = pl.ds(index * 1024, 1024)
        return pltpu.make_async_copy(raw.at[rows], out_hbm.at[rows], out_sem.at[index])

    @pl.loop(0, N // GROUP)
    def closing(index):
        last(index)
        save(index).start()

    for index in range(N // GROUP):
        save(index).wait()
    for flow in lead + rest:
        for stage, rows in enumerate((512, 384, 96, 24, 24, 96, 384, 512)):
            whole(flow, stage, rows).wait_send()


def local(quasi, outer_field, coupling):
    rows = quasi.reshape(4, ROWS, 128).transpose(1, 0, 2).reshape(4 * ROWS, 128)
    far = pl.BlockSpec(memory_space=pltpu.HBM)
    inside = pl.BlockSpec(memory_space=pltpu.VMEM)
    weights = [jnp.asarray(w) for w in tables()]
    shape = jax.ShapeDtypeStruct
    state = pltpu.VMEM((4, PADDED, 128), f32)
    field = pltpu.VMEM((ROWS, 128), f32)
    evolved, potentials = pl.pallas_call(
        kernel,
        out_shape=(shape((4 * ROWS, 128), f32), shape((3, 16, 128), f32)),
        in_specs=[far] * 8,
        out_specs=(far, inside),
        scratch_shapes=[
            pltpu.VMEM((4 * ROWS, 128), f32),
            pltpu.VMEM((3, ROWS, 128), f32),
            state,
            pltpu.VMEM((4, ROWS, 128), f32),
            state,
            state,
            pltpu.VMEM((3, ROWS, 128), f32),
            pltpu.VMEM((3, ROWS, 128), f32),
            pltpu.VMEM((6, 512, 128), f32),
            pltpu.VMEM((6, 384, 128), f32),
            pltpu.VMEM((6, 96, 128), f32),
            pltpu.VMEM((6, 24, 128), f32),
            field,
            field,
        ] + [pltpu.VMEM(w.shape, w.dtype) for w in weights] + [
            field,
            field,
            pltpu.VMEM((GROUP * 128, 128), f32),
            pltpu.SemaphoreType.DMA((4,)),
            pltpu.SemaphoreType.DMA((6, 8)),
            pltpu.SemaphoreType.DMA((6, 8)),
            pltpu.SemaphoreType.DMA((7,)),
            pltpu.SemaphoreType.DMA((N // GROUP,)),
        ],
        compiler_params=pltpu.CompilerParams(
            collective_id=0, has_side_effects=True, vmem_limit_bytes=VMEM_MIB * 2**20),
        name="superfluid",
    )(rows, outer_field.reshape(ROWS, 128), coupling.reshape(ROWS, 128), *weights)
    evolved = evolved.reshape(ROWS, 4, 128).transpose(1, 0, 2).reshape(1, 4, ROWS * 128)
    return evolved, potentials


def solution(mesh):
    return jax.shard_map(
        local,
        mesh=mesh,
        in_specs=(P(("grp", "wf"), None, None), P(), P()),
        out_specs=(P(("grp", "wf"), None, None), P(None, "grp", "wf")),
        check_vma=False,
    )
```

time: 78.7 us -> 62.6 us (0.80)
  Pallas kernels: 74 us -> 57.1 us
    pallas_call x2 -> x1, Pallas kernels: 74 us -> 57.1 us  [local(): pl.pallas_call(kernel, out_shape=(shape((4 * ROWS, 128), f32), shape((3,...]
where the time goes in v2:
time: 62.6 us; the launch traced here: 62.1 us
  Pallas kernels  57.1 us (91%)
  local copies, waits for them, and re-layouts  4.35 us (7%)
  between operations  0.65 us (1%)
    pallas_call x1, Pallas kernels, local(): pl.pallas_call(kernel, out_shape=(shape((4 * ROWS, 128), f32), shape((3,...  57.1 us
    unnamed x4, local copies, waits for them, and re-layouts  4.35 us

profile of v2, /device:TPU:1, one launch (start us, length us, event | category | flops | bytes accessed | tf_op | source)
XLA Modules:
  0.0 62.1 jit_solution(17888006065786255922)
XLA Ops:
  0.6 57.1 %superfluid.1 = (f32[8192,128]{1,0:T(8,128)}, f32[3,16,128]{2,1,0:T(8,128)}) custom-call(f32[8192,128]{1,0:T(8,128)} %bitcast.12, f32[2048,128]{1,0:T(8,128)} %bitcast.14, f32[2048,128]{1,0:T(8,128)} %bitcast.15, bf16[64,192]{1,0:T(8,128)(2,1)} %constant.10.clone.first_hbm, bf16[128,96]{1,0:T(8,128)(2,1)} %constant.11.clone.second_hbm, ...), custom_call_target="tpu_custom_call" | custom-call | tf_op jit(solution)/shard_map/superfluid/pallas_call | solution.py:418
  57.7 0.0 copy-start
  57.8 3.7 %copy.14 = f32[1,4,262144]{2,1,0:T(4,128)} copy(f32[1,4,262144]{2,1,0:T(4,128)} %bitcast.13) | data formatting | bytes 8388608
  61.5 0.0 copy-done
  61.5 0.6 copy.15
Async XLA Ops:
  57.7 3.8 %copy-start = (f32[3,16,128]{2,1,0:T(8,128)S(1)}, f32[3,16,128]{2,1,0:T(8,128)}, u32[]{:S(2)}) copy-start(f32[3,16,128]{2,1,0:T(8,128)} %get-tuple-element.9) | copy-start | bytes 73732

commit v3 on v2

--- a/solution.py
+++ b/solution.py
@@ -44,11 +44,10 @@
 
     high, low = cut(hartley)
     first = np.concatenate([high, high, low], axis=1)
-    blocks = [hartley[p::2, q::2] for p in range(2) for q in range(2)]
-    high, low = cut(np.concatenate(blocks, axis=0))
+    high, low = cut(np.concatenate([
+        np.concatenate([hartley[q::2, p::2] for p in range(2)], axis=1) for q in range(2)], axis=0))
     second = np.concatenate([high, high, low], axis=1)
-    third = np.kron(np.eye(2), np.concatenate([hartley, hartley], axis=0))
-    third = np.concatenate(cut(third), axis=0)
+    third = np.concatenate(cut(np.kron(np.eye(2), np.concatenate([hartley, hartley], axis=0))), axis=1)
     lane = np.arange(128)
     near = np.zeros((128, 128), np.float32)
     near[(lane & 64) | ((lane + 1) & 63), lane] += 1
@@ -88,16 +87,18 @@
 
 
 def kernel(q_hbm, outer_hbm, coupling_hbm, first_hbm, second_hbm, third_hbm, spectral_hbm, near_hbm,
-           out_hbm, potentials, raw, fields, start, laplace, ping, pong, part, full, met, got1, got2, got3,
+           out_hbm, potentials, raw, fields, start, laplace, ping, pong, part, full, met, got1, got2,
            outer, coupling, first, second, third, spectral, near, work, hill, beside,
            in_sem, send_sem, recv_sem, side_sem, out_sem):
     grp, wf = lax.axis_index("grp"), lax.axis_index("wf")
     core = grp % 2
     place = {"x": wf // 8, "y": wf % 4, "z": (wf // 4 % 2) * 2 + grp // 2}
 
-    def device(axis, shift):
+    def device(axis, shift, also=None, by=0):
         at = dict(place)
         at[axis] = (place[axis] + shift) % 4
+        if also:
+            at[also] = (place[also] + by) % 4
         return (at["z"] % 2 * 2 + core, at["x"] * 8 + at["z"] // 2 * 4 + at["y"])
 
     twin = (grp // 2 * 2 + 1 - core, wf)
@@ -111,12 +112,13 @@
         rows = pl.ds(pl.multiple_of(begin_of(piece) * 4, 8), 2048)
         return pltpu.make_async_copy(q_hbm.at[rows], raw.at[rows], in_sem.at[piece])
 
+    barrier = pltpu.get_barrier_semaphore()
+    partners = [device(axes[0], shift, axes[1], by) for axes in ("xy", "yz", "zx") for shift in (2, 1, 3) for by in (2, 1, 3)]
+    partners += [device(axis, shift) for axis in "xyz" for shift in (2, 1, 3)] + [twin]
+    for partner in partners:
+        pl.semaphore_signal(barrier, inc=1, device_id=partner, device_id_type=MESH)
     for piece in range(4):
         load(piece).start()
-    barrier = pltpu.get_barrier_semaphore()
-    partners = [twin] + [device(axis, shift) for axis in "xyz" for shift in (1, 2, 3)]
-    for partner in partners:
-        pl.semaphore_signal(barrier, inc=1, device_id=partner, device_id_type=MESH)
     tables_in = [
         pltpu.make_async_copy(source, target, side_sem.at[index])
         for index, (source, target) in enumerate((
@@ -181,90 +183,97 @@
             rows = pl.ds(pl.multiple_of(begin + step * 128, 8), 128)
             part[field, rows, :] = part[field, rows, :] + met[flow, pl.ds(step * 128, 128), :]
 
-        scatter(flow, 0)
-
-    def scatter(flow, level):
+        scatter(flow)
+
+    def scatter(flow):
         field, _, order = FLOWS[flow]
-        size = PARTS[level]
-        got = (got1, got2, got3)[level]
         for shift in (2, 1, 3):
-            peer = (place[order[level]] + shift) % 4
-            rows = pl.ds(pl.multiple_of(own(flow, level) + peer * size, 8), size)
-            send(flow, 1 + level, part.at[field, rows],
-                 got.at[flow, pl.ds((3 - shift) * size, size)], device(order[level], shift))
-
-    def add_axis(flow, level):
+            peer = (place[order[0]] + shift) % 4
+            rows = pl.ds(pl.multiple_of(own(flow, 0) + peer * 128, 8), 128)
+            send(flow, 1, part.at[field, rows], got1.at[flow, pl.ds((3 - shift) * 128, 128)], device(order[0], shift))
+
+    def each_peer(flow, call):
+        _, second_axis, third_axis = FLOWS[flow][2]
+
+        @pl.loop(1, 16)
+        def peers(index):
+            shifts = (index // 4, index % 4)
+            at = dict(place)
+            at[second_axis] = (place[second_axis] + shifts[0]) % 4
+            at[third_axis] = (place[third_axis] + shifts[1]) % 4
+            call(shifts, at[second_axis] * 32 + at[third_axis] * 8,
+                 (at["z"] % 2 * 2 + core, at["x"] * 8 + at["z"] // 2 * 4 + at["y"]))
+
+    def add_line(flow):
         field = FLOWS[flow][0]
-        size = PARTS[level]
-        got = (got1, got2, got3)[level]
-        begin = pl.multiple_of(own(flow, level + 1), 8)
-        arrived(flow, 1 + level, 3 * size)
-        rows = pl.ds(begin, size)
+        begin = pl.multiple_of(own(flow, 1), 8)
+        arrived(flow, 1, 384)
+        rows = pl.ds(begin, 128)
         total = part[field, rows, :]
         for slot in range(3):
-            total = total + got[flow, pl.ds(slot * size, size), :]
-        if level < 2:
-            part[field, rows, :] = total
-            scatter(flow, level + 1)
-        else:
-            full[field, rows, :] = total * (1.0 / 128.0)
-            spread(flow, 2)
-
-    def spread(flow, level):
+            total = total + got1[flow, pl.ds(slot * 128, 128), :]
+        part[field, rows, :] = total
+
+        def call(shifts, offset, to):
+            slot = (4 - shifts[0]) % 4 * 4 + (4 - shifts[1]) % 4 - 1
+            send(flow, 2, part.at[field, pl.ds(pl.multiple_of(begin + offset, 8), 8)],
+                 got2.at[flow, pl.ds(pl.multiple_of(slot * 8, 8), 8)], to)
+
+        each_peer(flow, call)
+
+    def add_layer(flow):
+        field = FLOWS[flow][0]
+        arrived(flow, 2, 120)
+        rows = pl.ds(pl.multiple_of(own(flow, 3), 8), 8)
+        terms = [part[field, rows, :]] + [got2[flow, pl.ds(slot * 8, 8), :] for slot in range(15)]
+        while len(terms) > 1:
+            terms = [terms[k] + terms[k + 1] for k in range(0, len(terms), 2)]
+        full[field, rows, :] = terms[0] * (1.0 / 128.0)
+        each_peer(flow, lambda shifts, offset, to: send(flow, 3, full.at[field, rows], full.at[field, rows], to))
+
+    def spread(flow):
         field, _, order = FLOWS[flow]
-        rows = pl.ds(pl.multiple_of(own(flow, level + 1), 8), PARTS[level])
+        arrived(flow, 3, 120)
+        rows = pl.ds(pl.multiple_of(own(flow, 1), 8), 128)
         for shift in (2, 1, 3):
-            send(flow, 6 - level, full.at[field, rows], full.at[field, rows],
-                 device(order[level], shift))
-
-    def gathered(flow, level):
-        arrived(flow, 6 - level, 3 * PARTS[level])
-        if level > 0:
-            spread(flow, level - 1)
-        else:
-            field = FLOWS[flow][0]
-            rows = pl.ds(pl.multiple_of(own(flow, 0), 8), 512)
-            send(flow, 7, full.at[field, rows], full.at[field, rows], twin)
+            send(flow, 4, full.at[field, rows], full.at[field, rows], device(order[0], shift))
+
+    def share(flow):
+        field = FLOWS[flow][0]
+        arrived(flow, 4, 384)
+        rows = pl.ds(pl.multiple_of(own(flow, 0), 8), 512)
+        send(flow, 5, full.at[field, rows], full.at[field, rows], twin)
 
     def thrice(values):
         high, low = high_low(values)
         return jnp.concatenate([high, low, high], axis=0)
 
-    def along_first(source, target, level):
-        @pl.loop(0, 2)
-        def columns(group):
-            for sub in range(4):
-                step = group * 4 + sub
-                slices = [pl.ds(step * 4 + k, N, stride=32) for k in range(4)]
-                values = jnp.concatenate([source[s, :] for s in slices], axis=1)
-                if level is not None:
-                    values = values - level
-                result = jnp.dot(first[...], thrice(values), preferred_element_type=f32)
-                for k in range(4):
-                    target[slices[k], :] = result[:, 128 * k:128 * k + 128]
-
-    def along_rest(source, target, weigh):
-        low_lanes = lax.broadcasted_iota(jnp.int32, (32, 128), 1) < 64
-
-        @pl.loop(0, 2)
-        def planes(group):
-            for sub in range(4):
-                base = pl.multiple_of((group * 4 + sub) * 256, 256)
-                values = jnp.concatenate([source[pl.ds(base + 32 * k, 32), :] for k in range(8)], axis=1)
-                mixed = jnp.dot(second[...], thrice(values), preferred_element_type=f32)
-                parts = []
-                for k in range(8):
-                    piece = mixed[:, 128 * k:128 * k + 128]
-                    parts.append(jnp.concatenate([
-                        jnp.where(low_lanes, piece[0:32], piece[32:64]),
-                        jnp.where(low_lanes, piece[64:96], piece[96:128])], axis=1))
-                high, low = high_low(jnp.concatenate(parts, axis=0))
-                result = jnp.dot(high, third[0:256, :], preferred_element_type=f32)
-                result = result + jnp.dot(low, third[0:256, :], preferred_element_type=f32)
-                result = result + jnp.dot(high, third[256:512, :], preferred_element_type=f32)
-                if weigh:
-                    result = result * spectral[pl.ds(base, 256), :]
-                target[pl.ds(base, 256), :] = result
+    def across_planes(source, target):
+        for step in range(8):
+            slices = [pl.ds(step * 4 + k, N, stride=32) for k in range(4)]
+            values = jnp.concatenate([source[s, :] for s in slices], axis=1)
+            values = jnp.dot(first[...], thrice(values), preferred_element_type=f32)
+            values = values * jnp.concatenate([spectral[s, :] for s in slices], axis=1)
+            values = jnp.dot(first[...], thrice(values), preferred_element_type=f32)
+            for k in range(4):
+                target[slices[k], :] = values[:, 128 * k:128 * k + 128]
+
+    even = jnp.where(lax.broadcasted_iota(jnp.int32, (32, 1024), 1) % 128 < 64, 1.0, 0.0).astype(bf16)
+
+    def within_planes(source, base, level=None):
+        values = jnp.concatenate([source[pl.ds(base + 32 * k, 32), :] for k in range(8)], axis=1)
+        if level is not None:
+            values = values - level
+        high, low = high_low(values)
+        high0, low0 = high * even, low * even
+        high1, low1 = high - high0, low - low0
+        mixed = jnp.dot(second[...], jnp.concatenate([high0, high1, low0, low1, high0, high1], axis=0),
+                        preferred_element_type=f32)
+        high, low = high_low(jnp.concatenate([
+            jnp.concatenate([mixed[0:32, 128 * k:128 * k + 128], mixed[32:64, 128 * k:128 * k + 128]], axis=1)
+            for k in range(8)], axis=0))
+        both = jnp.dot(high, third[...], preferred_element_type=f32)
+        return both[:, 0:128] + (both[:, 128:256] + jnp.dot(low, third[:, 0:128], preferred_element_type=f32))
 
     def prepare():
         @pl.loop(0, 32)
@@ -275,10 +284,10 @@
                         put(start, component, plane, block,
                             raw[pl.ds(plane * 128 + block * 32 + component, 8, stride=4), :])
 
-        tables_in[0].wait()
+    def opening_laplace(begin, end):
         upper = lax.broadcasted_iota(jnp.int32, (8, 128), 1) >= 64
 
-        @pl.loop(0, N // GROUP)
+        @pl.loop(begin, end)
         def groups(index):
             plane0 = index * GROUP
             beside_planes(start, near, beside, plane0)
@@ -304,48 +313,42 @@
     add_core(1)
     each(rest, add_core)
     prepare()
-    each(lead, add_axis, 0)
-    each(lead, add_axis, 1)
-    each(rest, add_axis, 0)
-    each(lead, add_axis, 2)
-    each(rest, add_axis, 1)
-    each(lead, gathered, 2)
-    each(rest, add_axis, 2)
-    each(lead, gathered, 1)
-    each(rest, gathered, 2)
-    each(lead, gathered, 0)
-    each(rest, gathered, 1)
-    for copy in tables_in[1:]:
+    for copy in tables_in:
         copy.wait()
-    each(lead, lambda flow: arrived(flow, 7, 512))
-    total = full[0, 0:64, :]
-    for index in range(1, 32):
-        total = total + full[0, 64 * index:64 * index + 64, :]
-    along_first(full.at[0], work, jnp.sum(total) * (1.0 / (ROWS * 128)))
-    along_rest(work, hill, True)
-    each(rest, gathered, 0)
-    along_rest(hill, work, False)
-    along_first(work, hill, None)
-    each(rest, lambda flow: arrived(flow, 7, 512))
-
-    @pl.loop(0, 32)
-    def fill(step):
-        for sub in range(8):
-            rows = pl.ds(pl.multiple_of(step * 64 + sub * 8, 8), 8)
-            scale = -2.0 * coupling[rows, :]
-            fields[0, rows, :] = 2.0 * (outer[rows, :] + full[0, rows, :] + hill[rows, :]) + 6.0
-            fields[1, rows, :] = scale * full[1, rows, :]
-            fields[2, rows, :] = scale * full[2, rows, :]
-
-    held = pl.ds(lax.axis_index("grp") * 512 + lax.axis_index("wf"), 16, stride=32)
-    potentials[0] = 0.5 * fields[0, held, :] - 3.0
-    potentials[1] = 0.5 * fields[1, held, :]
-    potentials[2] = 0.5 * fields[2, held, :]
+    each(lead, add_line)
+    opening_laplace(0, 3)
+    each(rest, add_line)
+    opening_laplace(3, 8)
+    each(lead, add_layer)
+    each(rest, add_layer)
+    each(lead, spread)
+    each(rest, spread)
+    each(lead, share)
+    mine = [pl.multiple_of(own(flow, 0) + part_row, 256) for flow in lead for part_row in (0, 256)]
+    other = [pl.multiple_of(base + 512 - 1024 * core, 256) for base in mine]
+    total = full[0, pl.ds(mine[0], 64), :]
+    for base in mine:
+        for row in range(0, 256, 64):
+            if base is not mine[0] or row:
+                total = total + full[0, pl.ds(base + row, 64), :]
+    level = jnp.sum(total) * (1.0 / (1024 * 128))
+    for base in mine:
+        work[pl.ds(base, 256), :] = within_planes(full.at[0], base, level)
+    each(lead, lambda flow: arrived(flow, 5, 512))
+    for base in other:
+        work[pl.ds(base, 256), :] = within_planes(full.at[0], base, level)
+    each(rest, share)
+    across_planes(work, hill)
+    for step in range(8):
+        rows = pl.ds(step * 256, 256)
+        fields[0, rows, :] = 2.0 * (outer[rows, :] + full[0, rows, :] + within_planes(hill, step * 256)) + 6.0
+    each(rest, lambda flow: arrived(flow, 5, 512))
+
     upper = lax.broadcasted_iota(jnp.int32, (8, 128), 1) >= 64
 
-    def combine(plane, block, state, total, factor, store):
+    def combine(plane, block, state, total, factor, store, held_fields=None):
         rows = pl.ds(pl.multiple_of(plane * 32, 32) + 8 * block, 8)
-        mean, real, imag = fields[0, rows, :], fields[1, rows, :], fields[2, rows, :]
+        mean, real, imag = held_fields or (fields[0, rows, :], fields[1, rows, :], fields[2, rows, :])
         a, b, c, d = state
         made = [mean * a - total[0] + (real * c - imag * d),
                 mean * b - total[1] + (real * d + imag * c),
@@ -383,10 +386,18 @@
             plane = index * 4 + sub
             for block in range(4):
                 rows = pl.ds(pl.multiple_of(plane * 32, 32) + 8 * block, 8)
+                scale = -2.0 * coupling[rows, :]
+                real, imag = scale * full[1, rows, :], scale * full[2, rows, :]
+                fields[1, rows, :] = real
+                fields[2, rows, :] = imag
                 state = [start[component, pl.ds(plane * PITCH + 8 + 8 * block, 8), :] for component in range(4)]
                 total = [laplace[component, rows, :] for component in range(4)]
-                combine(plane, block, state, total, time_step / 4, into(ping))
-
+                combine(plane, block, state, total, time_step / 4, into(ping), (fields[0, rows, :], real, imag))
+
+    held = pl.ds(lax.axis_index("grp") * 512 + lax.axis_index("wf"), 16, stride=32)
+    potentials[0] = 0.5 * fields[0, held, :] - 3.0
+    potentials[1] = 0.5 * fields[1, held, :]
+    potentials[2] = 0.5 * fields[2, held, :]
     for source, degree, target in ((ping, 3, pong), (pong, 2, ping)):
         pl.loop(0, N // GROUP)(step(source, time_step / degree, into(target)))
     last = step(ping, time_step, finish)
@@ -403,8 +414,23 @@
     for index in range(N // GROUP):
         save(index).wait()
     for flow in lead + rest:
-        for stage, rows in enumerate((512, 384, 96, 24, 24, 96, 384, 512)):
+        for stage, rows in enumerate((512, 384, 120, 120, 384, 512)):
             whole(flow, stage, rows).wait_send()
+
+
+def copy_kernel(evolved_in, potentials_in, evolved, potentials, lines, small, in_sem, out_sem):
+    pairs = [(evolved_in.at[rows], lines.at[rows], evolved.at[rows])
+             for rows in (pl.ds(index * 1024, 1024) for index in range(8))]
+    pairs.append((potentials_in, small, potentials))
+    arrive = [pltpu.make_async_copy(a, b, in_sem.at[index]) for index, (a, b, _) in enumerate(pairs)]
+    leave = [pltpu.make_async_copy(b, c, out_sem.at[index]) for index, (_, b, c) in enumerate(pairs)]
+    for copy in arrive:
+        copy.start()
+    for come, go in zip(arrive, leave):
+        come.wait()
+        go.start()
+    for copy in leave:
+        copy.wait()
 
 
 def local(quasi, outer_field, coupling):
@@ -431,8 +457,7 @@
             pltpu.VMEM((3, ROWS, 128), f32),
             pltpu.VMEM((6, 512, 128), f32),
             pltpu.VMEM((6, 384, 128), f32),
-            pltpu.VMEM((6, 96, 128), f32),
-            pltpu.VMEM((6, 24, 128), f32),
+            pltpu.VMEM((6, 120, 128), f32),
             field,
             field,
         ] + [pltpu.VMEM(w.shape, w.dtype) for w in weights] + [
@@ -440,8 +465,8 @@
             field,
             pltpu.VMEM((GROUP * 128, 128), f32),
             pltpu.SemaphoreType.DMA((4,)),
-            pltpu.SemaphoreType.DMA((6, 8)),
-            pltpu.SemaphoreType.DMA((6, 8)),
+            pltpu.SemaphoreType.DMA((6, 6)),
+            pltpu.SemaphoreType.DMA((6, 6)),
             pltpu.SemaphoreType.DMA((7,)),
             pltpu.SemaphoreType.DMA((N // GROUP,)),
         ],
@@ -449,6 +474,20 @@
             collective_id=0, has_side_effects=True, vmem_limit_bytes=VMEM_MIB * 2**20),
         name="superfluid",
     )(rows, outer_field.reshape(ROWS, 128), coupling.reshape(ROWS, 128), *weights)
+    evolved, potentials = pl.pallas_call(
+        copy_kernel,
+        out_shape=(shape((4 * ROWS, 128), f32), shape((3, 16, 128), f32)),
+        in_specs=[far] * 2,
+        out_specs=(far,) * 2,
+        scratch_shapes=[
+            pltpu.VMEM((4 * ROWS, 128), f32),
+            pltpu.VMEM((3, 16, 128), f32),
+            pltpu.SemaphoreType.DMA((9,)),
+            pltpu.SemaphoreType.DMA((9,)),
+        ],
+        compiler_params=pltpu.CompilerParams(vmem_limit_bytes=VMEM_MIB * 2**20),
+        name="deliver",
+    )(evolved, potentials)
     evolved = evolved.reshape(ROWS, 4, 128).transpose(1, 0, 2).reshape(1, 4, ROWS * 128)
     return evolved, potentials
 

time: 62.6 us -> 58.3 us (0.931)
  local copies, waits for them, and re-layouts: 4.35 us -> 0 us
    unnamed x4 -> x0, local copies, waits for them, and re-layouts: 4.35 us -> none
    pallas_call x0 -> x1, Pallas kernels: none -> 3.6 us  [local(): pl.pallas_call(copy_kernel, out_shape=(shape((4 * ROWS, 128), f32), shape...]
    pallas_call x1, Pallas kernels: 57.1 us -> 54 us  [local(): pl.pallas_call(kernel, out_shape=(shape((4 * ROWS, 128), f32), shape((3,...]
where the time goes in v3:
time: 58.3 us; the launch traced here: 58.2 us
  Pallas kernels  57.6 us (99%)
  between operations  0.64 us (1%)
    pallas_call x1, Pallas kernels, local(): pl.pallas_call(kernel, out_shape=(shape((4 * ROWS, 128), f32), shape((3,...  54 us
    pallas_call x1, Pallas kernels, local(): pl.pallas_call(copy_kernel, out_shape=(shape((4 * ROWS, 128), f32), shape...  3.6 us

profile of v3, /device:TPU:1, one launch (start us, length us, event | category | flops | bytes accessed | tf_op | source)
XLA Modules:
  0.0 58.2 jit_solution(2118535106205079550)
XLA Ops:
  0.6 54.0 %superfluid.1 = (f32[8192,128]{1,0:T(8,128)}, f32[3,16,128]{2,1,0:T(8,128)}) custom-call(f32[8192,128]{1,0:T(8,128)} %bitcast.12, f32[2048,128]{1,0:T(8,128)} %bitcast.13, f32[2048,128]{1,0:T(8,128)} %bitcast.14, bf16[64,192]{1,0:T(8,128)(2,1)} %constant.10.clone.first_hbm, bf16[64,192]{1,0:T(8,128)(2,1)} %constant.11.clone.second_hbm, ...), custom_call_target="tpu_custom_call" | custom-call | tf_op jit(solution)/shard_map/superfluid/pallas_call | solution.py:444
  54.6 3.6 %deliver.1 = (f32[8192,128]{1,0:T(8,128)}, f32[3,16,128]{2,1,0:T(8,128)}) custom-call(f32[8192,128]{1,0:T(8,128)} %get-tuple-element.6.evolved_in, f32[3,16,128]{2,1,0:T(8,128)} %get-tuple-element.7.potentials_in), custom_call_target="tpu_custom_call" | custom-call | tf_op jit(solution)/shard_map/deliver/pallas_call | solution.py:477

commit v4 on v3

--- a/solution.py
+++ b/solution.py
@@ -14,7 +14,7 @@
 HALF = 1024
 PITCH = 40
 PADDED = N * PITCH + 8
-GROUP = 8
+GROUP = 16
 VMEM_MIB = 58
 time_step = 0.2
 f32 = jnp.float32
@@ -94,11 +94,9 @@
     core = grp % 2
     place = {"x": wf // 8, "y": wf % 4, "z": (wf // 4 % 2) * 2 + grp // 2}
 
-    def device(axis, shift, also=None, by=0):
+    def device(axis, shift):
         at = dict(place)
         at[axis] = (place[axis] + shift) % 4
-        if also:
-            at[also] = (place[also] + by) % 4
         return (at["z"] % 2 * 2 + core, at["x"] * 8 + at["z"] // 2 * 4 + at["y"])
 
     twin = (grp // 2 * 2 + 1 - core, wf)
@@ -113,8 +111,7 @@
         return pltpu.make_async_copy(q_hbm.at[rows], raw.at[rows], in_sem.at[piece])
 
     barrier = pltpu.get_barrier_semaphore()
-    partners = [device(axes[0], shift, axes[1], by) for axes in ("xy", "yz", "zx") for shift in (2, 1, 3) for by in (2, 1, 3)]
-    partners += [device(axis, shift) for axis in "xyz" for shift in (2, 1, 3)] + [twin]
+    partners = [device(axis, shift) for axis in "xyz" for shift in (2, 1, 3)] + [twin]
     for partner in partners:
         pl.semaphore_signal(barrier, inc=1, device_id=partner, device_id_type=MESH)
     for piece in range(4):
@@ -207,7 +204,6 @@
     def add_line(flow):
         field = FLOWS[flow][0]
         begin = pl.multiple_of(own(flow, 1), 8)
-        arrived(flow, 1, 384)
         rows = pl.ds(begin, 128)
         total = part[field, rows, :]
         for slot in range(3):
@@ -299,7 +295,7 @@
                         laplace[component, rows, :] = neighbours(
                             start, beside, upper, plane, sub, component, 8 * block)[1]
 
-    lead, rest = (0, 1), (2, 3, 4, 5)
+    lead, rest = (0, 1), (2, 4, 3, 5)
 
     def each(flows, call, *levels):
         for flow in flows:
@@ -315,10 +311,13 @@
     prepare()
     for copy in tables_in:
         copy.wait()
+    each(lead, lambda flow: arrived(flow, 1, 384))
     each(lead, add_line)
-    opening_laplace(0, 3)
-    each(rest, add_line)
-    opening_laplace(3, 8)
+    opening_laplace(0, 2)
+    for flow in rest:
+        arrived(flow, 1, 384)
+        add_line(flow)
+    opening_laplace(2, 4)
     each(lead, add_layer)
     each(rest, add_layer)
     each(lead, spread)
@@ -342,8 +341,6 @@
     for step in range(8):
         rows = pl.ds(step * 256, 256)
         fields[0, rows, :] = 2.0 * (outer[rows, :] + full[0, rows, :] + within_planes(hill, step * 256)) + 6.0
-    each(rest, lambda flow: arrived(flow, 5, 512))
-
     upper = lax.broadcasted_iota(jnp.int32, (8, 128), 1) >= 64
 
     def combine(plane, block, state, total, factor, store, held_fields=None):
@@ -380,7 +377,6 @@
         for component in range(4):
             raw[pl.ds(plane * 128 + block * 32 + component, 8, stride=4), :] = values[component]
 
-    @pl.loop(0, N // 4)
     def opening(index):
         for sub in range(4):
             plane = index * 4 + sub
@@ -394,6 +390,9 @@
                 total = [laplace[component, rows, :] for component in range(4)]
                 combine(plane, block, state, total, time_step / 4, into(ping), (fields[0, rows, :], real, imag))
 
+    for half in range(2):
+        each(rest[2 * half:2 * half + 2], lambda flow: arrived(flow, 5, 512))
+        pl.loop(half * 8, half * 8 + 8)(opening)
     held = pl.ds(lax.axis_index("grp") * 512 + lax.axis_index("wf"), 16, stride=32)
     potentials[0] = 0.5 * fields[0, held, :] - 3.0
     potentials[1] = 0.5 * fields[1, held, :]
@@ -403,7 +402,7 @@
     last = step(ping, time_step, finish)
 
     def save(index):
-        rows = pl.ds(index * 1024, 1024)
+        rows = pl.ds(index * 2048, 2048)
         return pltpu.make_async_copy(raw.at[rows], out_hbm.at[rows], out_sem.at[index])
 
     @pl.loop(0, N // GROUP)

time: 58.3 us -> 56.5 us (0.969)
  Pallas kernels: 57.6 us -> 55.7 us
    pallas_call x1, Pallas kernels: 54 us -> 52.1 us  [local(): pl.pallas_call(kernel, out_shape=(shape((4 * ROWS, 128), f32), shape((3,...]
where the time goes in v4:
time: 56.5 us; the launch traced here: 56.3 us
  Pallas kernels  55.7 us (99%)
  between operations  0.64 us (1%)
    pallas_call x1, Pallas kernels, local(): pl.pallas_call(kernel, out_shape=(shape((4 * ROWS, 128), f32), shape((3,...  52.1 us
    pallas_call x1, Pallas kernels, local(): pl.pallas_call(copy_kernel, out_shape=(shape((4 * ROWS, 128), f32), shape...  3.6 us

profile of v4, /device:TPU:1, one launch (start us, length us, event | category | flops | bytes accessed | tf_op | source)
XLA Modules:
  0.0 56.3 jit_solution(9286086302918136618)
XLA Ops:
  0.6 52.1 %superfluid.1 = (f32[8192,128]{1,0:T(8,128)}, f32[3,16,128]{2,1,0:T(8,128)}) custom-call(f32[8192,128]{1,0:T(8,128)} %bitcast.12, f32[2048,128]{1,0:T(8,128)} %bitcast.13, f32[2048,128]{1,0:T(8,128)} %bitcast.14, bf16[64,192]{1,0:T(8,128)(2,1)} %constant.10.clone.first_hbm, bf16[64,192]{1,0:T(8,128)(2,1)} %constant.11.clone.second_hbm, ...), custom_call_target="tpu_custom_call" | custom-call | tf_op jit(solution)/shard_map/superfluid/pallas_call | solution.py:443
  52.7 3.6 %deliver.1 = (f32[8192,128]{1,0:T(8,128)}, f32[3,16,128]{2,1,0:T(8,128)}) custom-call(f32[8192,128]{1,0:T(8,128)} %get-tuple-element.6.evolved_in, f32[3,16,128]{2,1,0:T(8,128)} %get-tuple-element.7.potentials_in), custom_call_target="tpu_custom_call" | custom-call | tf_op jit(solution)/shard_map/deliver/pallas_call | solution.py:476

commit v5 on v4

--- a/solution.py
+++ b/solution.py
@@ -410,16 +410,16 @@
         last(index)
         save(index).start()
 
-    for index in range(N // GROUP):
-        save(index).wait()
     for flow in lead + rest:
         for stage, rows in enumerate((512, 384, 120, 120, 384, 512)):
             whole(flow, stage, rows).wait_send()
 
+    for index in range(N // GROUP):
+        save(index).wait()
 
 def copy_kernel(evolved_in, potentials_in, evolved, potentials, lines, small, in_sem, out_sem):
     pairs = [(evolved_in.at[rows], lines.at[rows], evolved.at[rows])
-             for rows in (pl.ds(index * 1024, 1024) for index in range(8))]
+             for rows in (pl.ds(index * 512, 512) for index in range(16))]
     pairs.append((potentials_in, small, potentials))
     arrive = [pltpu.make_async_copy(a, b, in_sem.at[index]) for index, (a, b, _) in enumerate(pairs)]
     leave = [pltpu.make_async_copy(b, c, out_sem.at[index]) for index, (_, b, c) in enumerate(pairs)]
@@ -481,8 +481,8 @@
         scratch_shapes=[
             pltpu.VMEM((4 * ROWS, 128), f32),
             pltpu.VMEM((3, 16, 128), f32),
-            pltpu.SemaphoreType.DMA((9,)),
-            pltpu.SemaphoreType.DMA((9,)),
+            pltpu.SemaphoreType.DMA((17,)),
+            pltpu.SemaphoreType.DMA((17,)),
         ],
         compiler_params=pltpu.CompilerParams(vmem_limit_bytes=VMEM_MIB * 2**20),
         name="deliver",

time: 56.5 us -> 56.7 us (level)
  no operation moved by 1% of the time
where the time goes in v5:
time: 56.7 us; the launch traced here: 56.6 us
  Pallas kernels  55.9 us (99%)
  between operations  0.64 us (1%)
    pallas_call x1, Pallas kernels, local(): pl.pallas_call(kernel, out_shape=(shape((4 * ROWS, 128), f32), shape((3,...  52 us
    pallas_call x1, Pallas kernels, local(): pl.pallas_call(copy_kernel, out_shape=(shape((4 * ROWS, 128), f32), shape...  3.87 us

profile of v5, /device:TPU:1, one launch (start us, length us, event | category | flops | bytes accessed | tf_op | source)
XLA Modules:
  0.0 56.6 jit_solution(6032847296735389505)
XLA Ops:
  0.6 52.0 %superfluid.1 = (f32[8192,128]{1,0:T(8,128)}, f32[3,16,128]{2,1,0:T(8,128)}) custom-call(f32[8192,128]{1,0:T(8,128)} %bitcast.12, f32[2048,128]{1,0:T(8,128)} %bitcast.13, f32[2048,128]{1,0:T(8,128)} %bitcast.14, bf16[64,192]{1,0:T(8,128)(2,1)} %constant.10.clone.first_hbm, bf16[64,192]{1,0:T(8,128)(2,1)} %constant.11.clone.second_hbm, ...), custom_call_target="tpu_custom_call" | custom-call | tf_op jit(solution)/shard_map/superfluid/pallas_call | solution.py:443
  52.7 3.9 %deliver.1 = (f32[8192,128]{1,0:T(8,128)}, f32[3,16,128]{2,1,0:T(8,128)}) custom-call(f32[8192,128]{1,0:T(8,128)} %get-tuple-element.6.evolved_in, f32[3,16,128]{2,1,0:T(8,128)} %get-tuple-element.7.potentials_in), custom_call_target="tpu_custom_call" | custom-call | tf_op jit(solution)/shard_map/deliver/pallas_call | solution.py:476
